TPU v7x, 32 devices: a whole 2x2x4 slice. The times are simulated.
32 devices in a mesh: gr: 4 (over y, core), gc: 8 (over z, x).
Axes of the slice: x: 2, y: 2, z: 4, core: 2. Of those that a mesh axis runs over, the one named last changes fastest.
Arguments:
- below_factor: bfloat16 [31, 4, 64, 2, 8, 128], P(None, 'gr', None, None, 'gc'), may hold values from -0.0625 to 0.0625
- panel_factor: bfloat16 [31, 4, 64, 512], P(None, 'gr', 'gc'), may hold values from -0.0625 to 0.0625
- prior_factor: bfloat16 [512, 2, 8, 128], P('gr', None, 'gc'), may hold values from -0.25 to 0.25
- diag_factor: float32 [512, 512], replicated, may hold values from -1 to 3, as said below
- diag_inverse: float32 [512, 512], replicated, may hold values from -2 to 1, as said below
- below_adjoint: bfloat16 [31, 4, 64, 2, 8, 128], P(None, 'gr', None, None, 'gc'), may hold values from -6 to 6
- panel_adjoint: bfloat16 [31, 4, 64, 512], P(None, 'gr', 'gc'), may hold values from -6 to 6
- prior_adjoint: bfloat16 [512, 2, 8, 128], P('gr', None, 'gc'), may hold values from -6 to 6
- diag_adjoint: float32 [512, 512], replicated, may hold values from -6 to 6
Outputs:
- below_update: bfloat16 [31, 4, 64, 2, 8, 128], P(None, 'gr', None, None, 'gc')
- panel_gradient: bfloat16 [31, 4, 64, 512], P(None, 'gr', 'gc')
- prior_update: bfloat16 [512, 2, 8, 128], P('gr', None, 'gc')
- diag_gradient: float32 [512, 512], replicated
Inputs may be any that keep to these rules, and one draw needn't show every extreme that they name: `diag_factor`: lower triangular, diagonal entries positive. `diag_inverse`: the inverse of diag_factor.
All inputs are finite; a program needn't handle non-finite values.
Results may differ from a plain program's by a relative error of at most 0.015.
Values may be sent and summed in bfloat16 or wider, within the bound.
No kernel may reach another device: no remote copies, remote signals or barrier semaphores. Data moves between devices by JAX's collectives and lax.ppermute only.
A program may use at most 64 MiB of HBM per device.

v0:
```python
import jax
import jax.numpy as jnp
from jax import lax
from jax.sharding import PartitionSpec as P


def row_product(left_rows, right_rows):
    return lax.dot_general(
        left_rows, right_rows, (((0,), (0,)), ((), ())), preferred_element_type=jnp.float32
    )


def diag_solve(diag_factor, diag_inverse, diag_reduced):
    highest = lax.Precision.HIGHEST
    chol_proj = jnp.dot(diag_factor.T, diag_reduced, precision=highest)
    phi_lower = jnp.tril(chol_proj) - 0.5 * jnp.diag(jnp.diagonal(chol_proj))
    symmetric = 0.5 * (phi_lower + phi_lower.T)
    left_side = jnp.dot(diag_inverse.T, symmetric, precision=highest)
    return jnp.dot(left_side, diag_inverse, precision=highest)


def local(
    below_factor,
    panel_factor,
    prior_factor,
    diag_factor,
    diag_inverse,
    below_adjoint,
    panel_adjoint,
    prior_adjoint,
    diag_adjoint,
):
    tile_count = below_factor.shape[0]
    tile_rows = below_factor.shape[2]
    local_rows = tile_count * tile_rows
    local_cols = below_factor.shape[3] * below_factor.shape[5]
    own_rows = panel_factor.shape[2]
    width = panel_factor.shape[3]
    prior_local = prior_factor.shape[0]
    below_mat = below_factor.reshape(local_rows, local_cols)
    below_bar = below_adjoint.reshape(local_rows, local_cols)
    inverse_bf = diag_inverse.astype(jnp.bfloat16)
    whole_bar, whole_factor = (
        lax.all_gather(panel_adjoint, "gc", axis=2, tiled=True),
        lax.all_gather(panel_factor, "gc", axis=2, tiled=True),
    )
    grad_rows = jnp.dot(
        whole_bar.reshape(local_rows, width), inverse_bf, preferred_element_type=jnp.float32
    ).astype(jnp.bfloat16)
    summed = lax.psum(
        row_product(grad_rows, whole_factor.reshape(local_rows, width)).astype(jnp.bfloat16), "gr"
    ).astype(jnp.float32)
    grid_col = lax.axis_index("gc")
    panel_grad = lax.dynamic_slice_in_dim(
        grad_rows.reshape(tile_count, 1, tile_rows, width), grid_col * own_rows, own_rows, 2
    )
    diag_reduced = jnp.tril(diag_adjoint - summed)
    diag_gradient = diag_solve(diag_factor, diag_inverse, diag_reduced)
    prior_here = prior_factor.reshape(prior_local, local_cols)
    prior_whole = lax.all_gather(prior_here, "gr", axis=0, tiled=True)
    below_new = (
        below_bar.astype(jnp.float32)
        - jnp.dot(grad_rows, prior_whole, preferred_element_type=jnp.float32)
    ).astype(jnp.bfloat16)
    crossing = lax.psum_scatter(
        row_product(grad_rows, below_mat).astype(jnp.bfloat16),
        "gr",
        scatter_dimension=0,
        tiled=True,
    ).astype(jnp.float32)
    grid_row = lax.axis_index("gr")
    twice_rows = lax.dynamic_slice_in_dim(
        2.0 * diag_gradient, grid_row * prior_local, prior_local, 0
    ).astype(jnp.bfloat16)
    curvature = jnp.dot(twice_rows, prior_whole, preferred_element_type=jnp.float32)
    prior_bar = prior_adjoint.reshape(prior_local, local_cols).astype(jnp.float32)
    prior_new = (prior_bar - crossing - curvature).astype(jnp.bfloat16)
    return (
        below_new.reshape(below_adjoint.shape),
        panel_grad,
        prior_new.reshape(prior_adjoint.shape),
        diag_gradient,
    )


def solution(mesh):
    in_specs = (
        P(None, "gr", None, None, "gc", None),
        P(None, "gr", "gc", None),
        P("gr", None, "gc", None),
        P(),
        P(),
        P(None, "gr", None, None, "gc", None),
        P(None, "gr", "gc", None),
        P("gr", None, "gc", None),
        P(),
    )
    out_specs = (
        P(None, "gr", None, None, "gc", None),
        P(None, "gr", "gc", None),
        P("gr", None, "gc", None),
        P(),
    )
    return jax.shard_map(local, mesh=mesh, in_specs=in_specs, out_specs=out_specs, check_vma=False)
```

profile of v0, /device:TPU:0, one launch (start us, length us, event | category | flops | bytes accessed | tf_op | source)
XLA Modules:
  0.0 179.4 jit_solution(4848968272577373393)
XLA Ops:
  7.2 0.0 copy-start
  7.2 0.0 all-gather.3.cloned.1.call-start
  7.2 0.7 all-gather.3.cloned.1.call-update
  7.9 0.0 all-gather.5.cloned.1.call-start
  8.0 0.7 all-gather.5.cloned.1.call-update
  8.7 0.0 all-reduce.2.cloned.1.call-start
  8.7 0.9 copy.32
  9.6 0.9 convert.3
  10.5 3.2 %convert.2 = f32[248,8,2,128]{3,2,1,0:T(2,128)} convert(bf16[248,8,2,128]{3,2,1,0:T(2,128)(2,1)} %bitcast.54) | non-fusion elementwise | flops 507904 | bytes 3047424
  13.7 7.2 %all_gather.10 = bf16[512,256]{1,0:T(8,128)(2,1)S(1)} all-gather(bf16[128,256]{1,0:T(8,128)(2,1)S(1)} %bitcast.56), channel_id=1, replica_groups=mesh['gr'=4,'gc'=8] {'gr'}, dimensions={0}, use_global_device_ids=true | all-gather | bytes 327680 | tf_op jit(solution)/shard_map/all_gather | solution.py:60
  20.9 42.1 %all-gather.3.cloned.1.call-done = bf16[31,1,64,512]{3,2,1,0:T(8,128)(2,1)} async-done(((bf16[31,1,8,512]{3,2,1,0:T(8,128)(2,1)}), bf16[31,1,64,512]{3,2,1,0:T(8,128)(2,1)}) %all-gather.3.cloned.1.call-update) | async-done | bytes 2031632 | tf_op jit(solution)/shard_map/all_gather | solution.py:44
  63.0 3.1 %convolution_convert_fusion = bf16[1984,512]{1,0:T(8,128)(2,1)S(1)} fusion(bf16[1984,512]{1,0:T(8,128)(2,1)} %bitcast.60, f32[512,512]{1,0:T(8,128)} %param.13), kind=kOutput, calls=%fused_computation.1 | convolution fusion | flops 1041465344 | bytes 5111808 | tf_op jit(solution)/shard_map/dot_general | solution.py:47
  66.1 47.5 %all-gather.5.cloned.1.call-done = bf16[31,1,64,512]{3,2,1,0:T(8,128)(2,1)} async-done(((bf16[31,1,8,512]{3,2,1,0:T(8,128)(2,1)}), bf16[31,1,64,512]{3,2,1,0:T(8,128)(2,1)}) %all-gather.5.cloned.1.call-update) | async-done | bytes 2031632 | tf_op jit(solution)/shard_map/all_gather | solution.py:45
  113.6 3.7 %convolution_convert_fusion.1 = bf16[512,512]{1,0:T(8,128)(2,1)} fusion(bf16[1984,512]{1,0:T(8,128)(2,1)S(1)} %convolution_convert_fusion, bf16[1984,512]{1,0:T(8,128)(2,1)} %bitcast.53), kind=kOutput, calls=%fused_computation.4 | convolution fusion | flops 1040449536 | bytes 4587520 | tf_op jit(solution)/shard_map/dot_general | solution.py:8
  117.2 0.0 all-reduce.2.cloned.1.call-update
  117.2 0.2 reduce-scatter.2.cloned.1.call-start
  117.5 3.2 %fusion = bf16[1984,256]{1,0:T(8,128)(2,1)} fusion(bf16[1984,512]{1,0:T(8,128)(2,1)S(1)} %convolution_convert_fusion, bf16[512,256]{1,0:T(8,128)(2,1)S(1)} %all_gather.10, f32[248,8,2,128]{3,2,1,0:T(2,128)} %convert.2), kind=kOutput, calls=%fused_computation.3 | convolution fusion | flops 521109504 | bytes 5341184 | tf_op jit(solution)/shard_map/dot_general | solution.py:63
  120.7 3.1 %reshape.38 = bf16[31,1,64,2,1,128]{5,3,2,0,4,1:T(2,128)(2,1)} reshape(bf16[1984,256]{1,0:T(8,128)(2,1)} %fusion) | data formatting | bytes 2031616 | tf_op jit(solution)/shard_map/reshape | solution.py:79
  123.7 0.7 constant_dynamic-slice_fusion
  124.5 2.7 %convolution_convert_fusion.2 = bf16[512,256]{1,0:T(8,128)(2,1)} fusion(bf16[1984,512]{1,0:T(8,128)(2,1)S(1)} %convolution_convert_fusion, bf16[248,8,2,128]{3,2,1,0:T(2,128)(2,1)} %bitcast.61), kind=kOutput, calls=%fused_computation.5 | convolution fusion | flops 520224768 | bytes 3309568 | tf_op jit(solution)/shard_map/dot_general | solution.py:8
  127.2 0.0 reduce-scatter.2.cloned.1.call-update
  127.2 21.6 %all-reduce.2.cloned.1.call-done = bf16[512,512]{1,0:T(8,128)(2,1)} async-done(((bf16[512,512]{1,0:T(8,128)(2,1)}), bf16[512,512]{1,0:T(8,128)(2,1)}) %all-reduce.2.cloned.1.call-update) | async-done | bytes 524304 | tf_op jit(solution)/shard_map/psum | solution.py:50
  148.7 0.0 copy-done
  148.8 3.2 %fusion.13 = f32[512,512]{1,0:T(8,128)S(1)} fusion(f32[512,512]{1,0:T(8,128)S(1)} %copy-done, f32[512,512]{1,0:T(8,128)} %param.17, bf16[512,512]{1,0:T(8,128)(2,1)} %all-reduce.2.cloned.1.call-done), kind=kOutput, calls=%fused_computation.22 | convolution fusion | flops 1611661312 | bytes 3670016 | tf_op jit(solution)/shard_map/dot_general | solution.py:15
  152.0 0.3 copy.18
  152.3 4.5 %gather_fusion = f32[512]{0:T(512)S(1)} fusion(f32[512,512]{1,0:T(8,128)S(1)} %bitcast.51, s32[512]{0:T(512)S(1)} %bitcast.50), kind=kCustom, calls=%fused_computation | custom fusion | bytes 8192 | tf_op jit(solution)/shard_map/jit(diagonal)/cond/branch_0_fun/gather | solution.py:16
  156.9 0.0 copy-start.2
  156.9 3.4 %fusion.2 = f32[512,512]{1,0:T(8,128)S(1)} fusion(f32[512,512]{1,0:T(8,128)} %param.13, f32[512,512]{1,0:T(8,128)S(1)} %fusion.13, f32[512]{0:T(512)S(1)} %gather_fusion, f32[512,512]{0,1:T(8,128)S(1)} %copy.18), kind=kOutput, calls=%fused_computation.8 | convolution fusion | flops 1614282752 | bytes 4196352 | tf_op jit(solution)/shard_map/dot_general | solution.py:18
  160.3 0.0 copy-done.2
  160.3 1.9 %fusion.34 = f32[512,512]{1,0:T(8,128)S(1)} fusion(f32[512,512]{1,0:T(8,128)S(1)} %fusion.2, f32[512,512]{1,0:T(8,128)S(1)} %copy-done.2), kind=kOutput, calls=%fused_computation.48 | convolution fusion | flops 1610612736 | bytes 3145728 | tf_op jit(solution)/shard_map/dot_general | solution.py:19
  162.2 0.0 copy-start.1
  162.2 8.9 %reduce-scatter.2.cloned.1.call-done = bf16[128,256]{1,0:T(8,128)(2,1)} async-done(((bf16[512,256]{1,0:T(8,128)(2,1)}), bf16[128,256]{1,0:T(8,128)(2,1)}) %reduce-scatter.2.cloned.1.call-update) | async-done | bytes 65552 | tf_op jit(solution)/shard_map/reduce_scatter | solution.py:65
  171.1 1.0 fusion.1
  172.2 0.7 reshape.42
  172.8 0.0 copy-done.1
  (1 shorter events, 0.0 us)
Async XLA Ops:
  7.2 141.6 %copy-start = (f32[512,512]{1,0:T(8,128)S(1)}, f32[512,512]{1,0:T(8,128)}, u32[]{:S(2)}) copy-start(f32[512,512]{1,0:T(8,128)} %param.12) | copy-start | bytes 3145732
  7.2 55.9 %all-gather.3.cloned.1.call-start = ((), (), s32[]{:S(2)}) async-start(), calls=%async_computation.1 | async-start | bytes 2285568 | tf_op jit(solution)/shard_map/all_gather | solution.py:44
  7.9 105.7 %all-gather.5.cloned.1.call-start = ((), (), s32[]{:S(2)}) async-start(), calls=%async_computation.3 | async-start | bytes 2285568 | tf_op jit(solution)/shard_map/all_gather | solution.py:45
  8.7 140.1 %all-reduce.2.cloned.1.call-start = ((), (), s32[]{:S(2)}) async-start(), calls=%async_computation.4 | async-start | bytes 1048576 | tf_op jit(solution)/shard_map/psum | solution.py:50
  117.2 53.9 %reduce-scatter.2.cloned.1.call-start = ((), (), s32[]{:S(2)}) async-start(), calls=%async_computation.2 | async-start | bytes 327680 | tf_op jit(solution)/shard_map/reduce_scatter | solution.py:65
  156.9 3.4 %copy-start.2 = (f32[512,512]{1,0:T(8,128)S(1)}, f32[512,512]{1,0:T(8,128)}, u32[]{:S(2)}) copy-start(f32[512,512]{1,0:T(8,128)} %param.13) | copy-start | bytes 3145732
  162.2 10.6 %copy-start.1 = (f32[512,512]{1,0:T(8,128)}, f32[512,512]{1,0:T(8,128)S(1)}, u32[]{:S(2)}) copy-start(f32[512,512]{1,0:T(8,128)S(1)} %fusion.34) | copy-start | bytes 3145732
Sparse Core Ops, SparseCore 0:
  10.1 52.9 all-gather.2
  65.1 48.4 all-gather.4
  117.4 31.3 all-reduce.1
  151.1 20.0 reduce-scatter.1
where the time goes:
time: 180 us; the launch traced here: 179 us
  waiting for transfers between devices  121 us (67%)
  matrix products  22.2 us (12%)
  between operations  13.9 us (8%)
  local copies, waits for them, and re-layouts  10.1 us (6%)
  blocking collectives  7.21 us (4%)
  other arithmetic  4.13 us (2%)
    all_gather x1, waiting for transfers between devices, local(): lax.all_gather(panel_factor, 'gc', axis=2, tiled=True)  47.5 us
    all_gather x1, waiting for transfers between devices, local(): lax.all_gather(panel_adjoint, 'gc', axis=2, tiled=True)  42.1 us
    psum x1, waiting for transfers between devices, local(): lax.psum(row_product(grad_rows, whole_factor.reshape(local_rows, width))....  21.6 us
    reduce_scatter x1, waiting for transfers between devices, local(): lax.psum_scatter(row_product(grad_rows, below_mat).astype(jnp.bfloat16),...  8.93 us
    all_gather x1, blocking collectives, local(): prior_whole = lax.all_gather(prior_here, 'gr', axis=0, tiled=True)  7.21 us
    dot_general x2, matrix products, row_product(): lax.dot_general(left_rows, right_rows, (((0,), (0,)), ((), ())), preferre...  6.36 us
    gather x1, local copies, waits for them, and re-layouts, diag_solve(): phi_lower = jnp.tril(chol_proj) - 0.5 * jnp.diag(jnp.diagonal(chol_proj))  4.52 us
    unnamed x2, other arithmetic  4.12 us
  transfers between devices with their start and end apart: 4, of which 4 were waited for; matrix products, arithmetic and copies ran while one was open for 17% of the time, Pallas kernels for 0%

commit v1 on v0

v1 whole, which is shorter than its diff:
```python
import functools

import jax
import jax.numpy as jnp
from jax import lax
from jax.experimental import pallas as pl
from jax.experimental.pallas import tpu as pltpu
from jax.sharding import PartitionSpec as P

BF = jnp.bfloat16
F32 = jnp.float32
BLK = 128


def row_product(left_rows, right_rows):
    return lax.dot_general(
        left_rows, right_rows, (((0,), (0,)), ((), ())), preferred_element_type=F32
    )


def diag_solve(diag_factor, diag_inverse, diag_reduced):
    highest = lax.Precision.HIGHEST
    chol_proj = jnp.dot(diag_factor.T, diag_reduced, precision=highest)
    phi_lower = jnp.tril(chol_proj) - 0.5 * jnp.diag(jnp.diagonal(chol_proj))
    symmetric = 0.5 * (phi_lower + phi_lower.T)
    left_side = jnp.dot(diag_inverse.T, symmetric, precision=highest)
    return jnp.dot(left_side, diag_inverse, precision=highest)


def local_any(
    below_factor,
    panel_factor,
    prior_factor,
    diag_factor,
    diag_inverse,
    below_adjoint,
    panel_adjoint,
    prior_adjoint,
    diag_adjoint,
):
    tile_count = below_factor.shape[0]
    tile_rows = below_factor.shape[2]
    local_rows = tile_count * tile_rows
    local_cols = below_factor.shape[3] * below_factor.shape[5]
    own_rows = panel_factor.shape[2]
    width = panel_factor.shape[3]
    prior_local = prior_factor.shape[0]
    below_mat = below_factor.reshape(local_rows, local_cols)
    below_bar = below_adjoint.reshape(local_rows, local_cols)
    inverse_bf = diag_inverse.astype(BF)
    own_grad = jnp.dot(
        panel_adjoint.reshape(tile_count * own_rows, width),
        inverse_bf,
        preferred_element_type=F32,
    ).astype(BF)
    summed = lax.psum(
        row_product(own_grad, panel_factor.reshape(tile_count * own_rows, width)).astype(BF),
        ("gr", "gc"),
    ).astype(F32)
    panel_grad = own_grad.reshape(panel_adjoint.shape)
    grad_rows = lax.all_gather(panel_grad, "gc", axis=2, tiled=True).reshape(local_rows, width)
    diag_reduced = jnp.tril(diag_adjoint - summed)
    diag_gradient = diag_solve(diag_factor, diag_inverse, diag_reduced)
    prior_here = prior_factor.reshape(prior_local, local_cols)
    prior_whole = lax.all_gather(prior_here, "gr", axis=0, tiled=True)
    below_new = (
        below_bar.astype(F32) - jnp.dot(grad_rows, prior_whole, preferred_element_type=F32)
    ).astype(BF)
    crossing = lax.psum_scatter(
        row_product(grad_rows, below_mat).astype(BF), "gr", scatter_dimension=0, tiled=True
    ).astype(F32)
    twice_rows = lax.dynamic_slice_in_dim(
        2.0 * diag_gradient, lax.axis_index("gr") * prior_local, prior_local, 0
    ).astype(BF)
    curvature = jnp.dot(twice_rows, prior_whole, preferred_element_type=F32)
    prior_bar = prior_adjoint.reshape(prior_local, local_cols).astype(F32)
    prior_new = (prior_bar - crossing - curvature).astype(BF)
    return (
        below_new.reshape(below_adjoint.shape),
        panel_grad,
        prior_new.reshape(prior_adjoint.shape),
        diag_gradient,
    )


VM = pl.BlockSpec(memory_space=pltpu.VMEM)


def call(body, outs, ins, scratch=(), flops=0, nbytes=0, name=None):
    return pl.pallas_call(
        body,
        out_shape=[jax.ShapeDtypeStruct(s, d) for s, d in outs],
        in_specs=[VM] * len(ins),
        out_specs=[VM] * len(outs),
        scratch_shapes=list(scratch),
        compiler_params=pltpu.CompilerParams(vmem_limit_bytes=40 * 2**20),
        cost_estimate=pl.CostEstimate(flops=flops, bytes_accessed=nbytes, transcendentals=0),
        name=name,
    )(*ins)


def lower_blocks(count):
    return [(r, c) for r in range(count) for c in range(r + 1)]


def my_core():
    return lax.rem(lax.axis_index("gr"), 2)


def my_y():
    return lax.div(lax.axis_index("gr"), 2)


def grad_kernel(adj, fac, inv, grad, keep, send):
    grad_bf = jnp.dot(adj[...], inv[...].astype(BF), preferred_element_type=F32).astype(BF)
    grad[...] = grad_bf
    blocks = lower_blocks(adj.shape[1] // BLK)
    half = len(blocks) // 2
    core = my_core()
    for row in range(adj.shape[1] // BLK):
        strip = row_product(
            grad_bf[:, row * BLK : (row + 1) * BLK], fac[:, : (row + 1) * BLK]
        )
        for col in range(row + 1):
            at = blocks.index((row, col))
            which, place = at // half, at % half
            piece = strip[:, col * BLK : (col + 1) * BLK]
            here = pl.ds(place * BLK, BLK)

            @pl.when(core == which)
            def _():
                keep[here, :] = piece

            @pl.when(core != which)
            def _():
                send[here, :] = piece.astype(BF)


def split(value):
    high = value.astype(BF)
    return high, (value - high.astype(F32)).astype(BF)


def prep_kernel(fac, inv, fac_t_hi, fac_t_lo, inv_t_hi, inv_t_lo, inv_hi, inv_lo):
    fac_t_hi[...], fac_t_lo[...] = split(fac[...].T)
    inverse = inv[...]
    inv_t_hi[...], inv_t_lo[...] = split(inverse.T)
    inv_hi[...], inv_lo[...] = split(inverse)


def dot3(a_hi, a_lo, b):
    b_hi, b_lo = split(b)
    d = functools.partial(jnp.dot, preferred_element_type=F32)
    return d(a_hi, b_hi) + (d(a_lo, b_hi) + d(a_hi, b_lo))


def dot3r(a, b_hi, b_lo):
    a_hi, a_lo = split(a)
    d = functools.partial(jnp.dot, preferred_element_type=F32)
    return d(a_hi, b_hi) + (d(a_lo, b_hi) + d(a_hi, b_lo))


def natural(view, scratch):
    rows = view.shape[0] // 2
    scratch[...] = view.astype(F32)
    return jnp.concatenate(
        [scratch[pl.ds(t, rows, stride=2), :] for t in range(2)], axis=1
    ).astype(BF)


def place_quarters(refs, store):
    core, y = my_core(), my_y()
    for k, ref in enumerate(refs):
        store(jnp.bitwise_xor(y, k % 2), jnp.bitwise_xor(core, k // 2), ref)


def natural_prior(refs, scratch, whole):
    def put(y, core, ref):
        at = pl.multiple_of((2 * y + core) * BLK, BLK)
        whole[pl.ds(at, BLK), :] = natural(ref[...], scratch)

    place_quarters(refs, put)


def solve_kernel(
    c0, c1, c2, c3, p0, p1, p2, p3, bar, dadj,
    fac_t_hi, fac_t_lo, inv_t_hi, inv_t_lo, inv_hi, inv_lo,
    out, rest, cross, whole, twice, inter,
):
    quarter = c0.shape[0]

    def put(y, core, ref):
        at = pl.multiple_of((2 * core + y) * quarter, quarter)
        cross[pl.ds(at, quarter), :] = ref[...].astype(F32)

    place_quarters((c0, c1, c2, c3), put)
    natural_prior((p0, p1, p2, p3), inter, whole)
    size = dadj.shape[0]
    count = size // BLK
    blocks = lower_blocks(count)
    zero = jnp.zeros((BLK, BLK), F32)
    strips = []
    for row in range(count):
        parts = []
        for col in range(count):
            if col > row:
                parts.append(zero)
            else:
                at = blocks.index((row, col))
                parts.append(
                    dadj[row * BLK : (row + 1) * BLK, col * BLK : (col + 1) * BLK]
                    - cross[at * BLK : (at + 1) * BLK, :]
                )
        strips.append(jnp.concatenate(parts, axis=1))
    reduced = jnp.concatenate(strips, axis=0)
    r_at = lax.broadcasted_iota(jnp.int32, (size, size), 0)
    c_at = lax.broadcasted_iota(jnp.int32, (size, size), 1)
    reduced = jnp.where(r_at >= c_at, reduced, 0.0)
    proj = dot3(fac_t_hi[...], fac_t_lo[...], reduced)
    phi = jnp.where(r_at > c_at, proj, jnp.where(r_at == c_at, 0.5 * proj, 0.0))
    left = dot3(inv_t_hi[...], inv_t_lo[...], phi)
    full = dot3r(left, inv_hi[...], inv_lo[...])
    grad = 0.5 * (full + full.T)
    out[...] = grad
    twice[...] = 2.0 * grad
    own = pl.multiple_of(lax.axis_index("gr") * BLK, BLK)
    rows = twice[pl.ds(own, BLK), :].astype(BF)
    curvature = jnp.dot(rows, whole[...], preferred_element_type=F32)
    inter[...] = bar[...].astype(F32)
    prior_bar = jnp.concatenate(
        [inter[pl.ds(t, BLK, stride=2), :] for t in range(2)], axis=1
    )
    rest[...] = prior_bar - curvature


def final_kernel(rest, keep, recv, out, inter):
    value = rest[...] - (keep[...] + recv[...].astype(F32))
    for t in range(2):
        inter[pl.ds(t, BLK, stride=2), :] = value[:, t * BLK : (t + 1) * BLK]
    out[...] = inter[...].astype(BF)


def ring_order(n):
    return list(range(0, n, 2)) + list(range(n - 1, 0, -2))


def shard_of(offset, n):
    me = lax.axis_index("gc")
    half = lax.div(me, 2)
    pos = jnp.where(lax.rem(me, 2) == 0, half, n - 1 - half)
    at = lax.rem(pos - offset + 2 * n, n)
    return jnp.where(at < n // 2, 2 * at, 2 * (n - 1 - at) + 1)


def crossing_kernel(offsets, n, *refs):
    grads = refs[: len(offsets)]
    below, keep, send, inter, acc = refs[len(offsets) :]
    for k, off in enumerate(offsets):
        j = shard_of(off, n)
        view = below[:, j]
        rows = natural(view.reshape(view.shape[0] * view.shape[1], view.shape[2]), inter)
        part = row_product(grads[k][...], rows)
        if k == 0:
            acc[...] = part
        else:
            acc[...] += part
    core = my_core()
    for which in range(2):
        for y in range(2):
            piece = acc[(2 * y + which) * BLK : (2 * y + which + 1) * BLK, :]

            @pl.when(core == which)
            def _():
                keep[y] = piece

            @pl.when(core != which)
            def _():
                send[y] = piece.astype(BF)


def below_kernel(offsets, n, *refs):
    grads = refs[: len(offsets)]
    p0, p1, p2, p3, bar, out, inter, small, whole = refs[len(offsets) :]
    natural_prior((p0, p1, p2, p3), small, whole)
    for k, off in enumerate(offsets):
        j = shard_of(off, n)
        prod = jnp.dot(grads[k][...], whole[...], preferred_element_type=F32)
        for t in range(2):
            inter[pl.ds(t, prod.shape[0], stride=2), :] = prod[:, t * BLK : (t + 1) * BLK]
        view = bar[:, j]
        old = view.reshape(view.shape[0] * view.shape[1], view.shape[2]).astype(F32)
        out[:, j] = (old - inter[...]).astype(BF).reshape(view.shape)


def xor_perm(n, bit):
    return [(i, i ^ bit) for i in range(n)]


def local_fast(
    below_factor,
    panel_factor,
    prior_factor,
    diag_factor,
    diag_inverse,
    below_adjoint,
    panel_adjoint,
    prior_adjoint,
    diag_adjoint,
    n_gr,
    n_gc,
):
    tiles, _, tile_rows, ct, _, cb = below_factor.shape
    own_rows, width = panel_factor.shape[2:]
    shard_rows = tiles * own_rows
    cols = ct * cb
    prior_local = prior_factor.shape[0]
    core = lambda v: lax.ppermute(v, "gr", xor_perm(n_gr, 1))
    ynb = lambda v: lax.ppermute(v, "gr", xor_perm(n_gr, 2))
    gcx = lambda v, bit: lax.ppermute(v, "gc", xor_perm(n_gc, bit))
    cyc = ring_order(n_gc)
    right = [(cyc[i], cyc[(i + 1) % n_gc]) for i in range(n_gc)]
    left = [(b, a) for a, b in right]

    bf_view = below_factor.reshape(tiles, n_gc, own_rows * ct, cb)
    ba_view = below_adjoint.reshape(tiles, n_gc, own_rows * ct, cb)
    pf_view = prior_factor.reshape(prior_local * ct, cb)
    pa_view = prior_adjoint.reshape(prior_local * ct, cb)

    n_blocks = len(lower_blocks(width // BLK))
    half_rows = n_blocks // 2 * BLK
    quarter = half_rows // 2
    grad, keep, send = call(
        grad_kernel,
        [((shard_rows, width), BF), ((half_rows, BLK), F32), ((half_rows, BLK), BF)],
        [
            panel_adjoint.reshape(shard_rows, width),
            panel_factor.reshape(shard_rows, width),
            diag_inverse,
        ],
        flops=4 * shard_rows * width * width,
        nbytes=2**21,
        name="panel_grad",
    )

    got = core(send)
    y = my_y()
    both = (keep + got.astype(F32)).reshape(2, quarter, BLK)
    mine = lax.dynamic_index_in_dim(both, y, 0, keepdims=False)
    other = lax.dynamic_index_in_dim(both, 1 - y, 0, keepdims=False).astype(BF)
    part = (mine + ynb(other).astype(F32)).astype(BF)
    part = (part.astype(F32) + gcx(part, 1).astype(F32)).astype(BF)
    p2, p4, p6 = gcx(part, 2), gcx(part, 4), gcx(part, 6)
    part = (
        (part.astype(F32) + p2.astype(F32)) + (p4.astype(F32) + p6.astype(F32))
    ).astype(BF)
    part_y = ynb(part)
    part_c = core(part)
    part_b = core(part_y)

    grads, offsets = [grad], [0]
    r = l = grad
    for step in range(1, n_gc // 2 + 1):
        r = lax.ppermute(r, "gc", right)
        grads.append(r)
        offsets.append(step)
        if step < n_gc - step:
            l = lax.ppermute(l, "gc", left)
            grads.append(l)
            offsets.append(-step)

    pf_y = ynb(pf_view)
    pf_c = core(pf_view)
    pf_b = core(pf_y)
    priors = [pf_view, pf_y, pf_c, pf_b]

    prepared = call(
        prep_kernel,
        [((width, width), BF)] * 6,
        [diag_factor, diag_inverse],
        flops=10 * width * width,
        nbytes=2**22,
        name="prep",
    )

    keep_x, send_x = call(
        functools.partial(crossing_kernel, offsets, n_gc),
        [((2, BLK, cols), F32), ((2, BLK, cols), BF)],
        [*grads, bf_view],
        scratch=[
            pltpu.VMEM((shard_rows * ct, cb), F32),
            pltpu.VMEM((width, cols), F32),
        ],
        flops=2 * shard_rows * n_gc * width * cols,
        nbytes=2**22,
        name="crossing",
    )
    both_x = keep_x + core(send_x).astype(F32)
    mine_x = lax.dynamic_index_in_dim(both_x, y, 0, keepdims=False)
    other_x = lax.dynamic_index_in_dim(both_x, 1 - y, 0, keepdims=False).astype(BF)
    got_x = ynb(other_x)

    (below_new,) = call(
        functools.partial(below_kernel, offsets, n_gc),
        [(ba_view.shape, BF)],
        [*grads, *priors, ba_view],
        scratch=[
            pltpu.VMEM((shard_rows * ct, cb), F32),
            pltpu.VMEM((prior_local * ct, cb), F32),
            pltpu.VMEM((width, cols), BF),
        ],
        flops=2 * shard_rows * n_gc * width * cols,
        nbytes=2**22,
        name="below",
    )

    diag_gradient, rest = call(
        solve_kernel,
        [((width, width), F32), ((prior_local, cols), F32)],
        [part, part_y, part_c, part_b, *priors, pa_view, diag_adjoint, *prepared],
        scratch=[
            pltpu.VMEM((n_blocks * BLK, BLK), F32),
            pltpu.VMEM((width, cols), BF),
            pltpu.VMEM((width, width), F32),
            pltpu.VMEM((prior_local * ct, cb), F32),
        ],
        flops=18 * width**3,
        nbytes=2**22,
        name="solve",
    )
    (prior_new,) = call(
        final_kernel,
        [(pa_view.shape, BF)],
        [rest, mine_x, got_x],
        scratch=[pltpu.VMEM((prior_local * ct, cb), F32)],
        flops=10 * prior_local * cols,
        nbytes=2**18,
        name="prior_sum",
    )
    return (
        below_new.reshape(below_adjoint.shape),
        grad.reshape(panel_adjoint.shape),
        prior_new.reshape(prior_adjoint.shape),
        diag_gradient,
    )


def solution(mesh):
    n_gr, n_gc = mesh.shape["gr"], mesh.shape["gc"]

    def local(*args):
        below_factor, panel_factor, prior_factor = args[:3]
        fits = (
            n_gr == 4
            and n_gc == 8
            and panel_factor.shape[2] == 8
            and below_factor.shape[3] == 2
            and below_factor.shape[5] == BLK
            and prior_factor.shape[0] == BLK
        )
        if fits:
            return local_fast(*args, n_gr=n_gr, n_gc=n_gc)
        return local_any(*args)

    in_specs = (
        P(None, "gr", None, None, "gc", None),
        P(None, "gr", "gc", None),
        P("gr", None, "gc", None),
        P(),
        P(),
        P(None, "gr", None, None, "gc", None),
        P(None, "gr", "gc", None),
        P("gr", None, "gc", None),
        P(),
    )
    out_specs = (
        P(None, "gr", None, None, "gc", None),
        P(None, "gr", "gc", None),
        P("gr", None, "gc", None),
        P(),
    )
    return jax.shard_map(local, mesh=mesh, in_specs=in_specs, out_specs=out_specs, check_vma=False)
```

time: 180 us -> 58.9 us (0.33)
  the two profiles are of different devices: /device:TPU:0 before, /device:TPU:2 now
where the time goes in v1:
time: 58.9 us; the launch traced here: 58.7 us
  waiting for transfers between devices  25.7 us (44%)
  starting transfers between devices  18.7 us (32%)
  Pallas kernels  10 us (17%)
  local copies, waits for them, and re-layouts  3.29 us (6%)
  between operations  0.81 us (1%)
    pallas_call x6, Pallas kernels, call(): pl.pallas_call(body, out_shape=[jax.ShapeDtypeStruct(s, d) for s, d in ou...  10 us
    ppermute x4, waiting for transfers between devices, local_fast(): gcx = lambda v, bit: lax.ppermute(v, 'gc', xor_perm(n_gc, bit))  8.54 us
    ppermute x4, waiting for transfers between devices, local_fast(): r = lax.ppermute(r, 'gc', right)  8.28 us
    ppermute x4, waiting for transfers between devices, local_fast(): ynb = lambda v: lax.ppermute(v, 'gr', xor_perm(n_gr, 2))  7.3 us
    ppermute x4, starting transfers between devices, local_fast(): gcx = lambda v, bit: lax.ppermute(v, 'gc', xor_perm(n_gc, bit))  6.86 us
    ppermute x4, starting transfers between devices, local_fast(): ynb = lambda v: lax.ppermute(v, 'gr', xor_perm(n_gr, 2))  4.61 us
    ppermute x3, starting transfers between devices, local_fast(): l = lax.ppermute(l, 'gc', left)  4.54 us
    unnamed x22, local copies, waits for them, and re-layouts  3.24 us
  transfers between devices with their start and end apart: 21, of which 10 were waited for; matrix products, arithmetic and copies ran while one was open for 0% of the time, Pallas kernels for 13%

profile of v1, /device:TPU:2, one launch (start us, length us, event | category | flops | bytes accessed | tf_op | source)
XLA Modules:
  0.0 58.7 jit_solution(10679892858712204306)
XLA Ops:
  0.6 0.0 copy-start
  0.6 1.2 %copy-done = f32[512,512]{1,0:T(8,128)S(1)} copy-done((f32[512,512]{1,0:T(8,128)S(1)}, f32[512,512]{1,0:T(8,128)}, u32[]{:S(2)}) %copy-start) | copy-done | bytes 1048600
  1.9 0.0 copy-start.6
  1.9 0.9 %copy-done.6 = bf16[31,1,8,512]{3,2,1,0:T(8,128)(2,1)S(1)} copy-done((bf16[31,1,8,512]{3,2,1,0:T(8,128)(2,1)S(1)}, bf16[31,1,8,512]{3,2,1,0:T(8,128)(2,1)}, u32[]{:S(2)}) %copy-start.6) | copy-done | bytes 253976
  2.8 0.9 %copy-done.7 = bf16[31,1,8,512]{3,2,1,0:T(8,128)(2,1)S(1)} copy-done((bf16[31,1,8,512]{3,2,1,0:T(8,128)(2,1)S(1)}, bf16[31,1,8,512]{3,2,1,0:T(8,128)(2,1)}, u32[]{:S(2)}) %copy-start.7) | copy-done | bytes 253976
  3.8 1.8 %panel_grad.1 = (bf16[248,512]{1,0:T(8,128)(2,1)}, f32[640,128]{1,0:T(8,128)S(1)}, bf16[640,128]{1,0:T(8,128)(2,1)S(1)}) custom-call(bf16[248,512]{1,0:T(8,128)(2,1)S(1)} %bitcast.29, bf16[248,512]{1,0:T(8,128)(2,1)S(1)} %bitcast.30, f32[512,512]{1,0:T(8,128)S(1)} %copy-done), custom_call_target="tpu_custom_call" | custom-call | flops 260046848 | bytes 2097152 | tf_op jit(solution)/shard_map/panel_grad/pallas_call | solution.py:90
  5.6 0.0 collective-permute-start.10
  5.6 0.0 collective-permute-start
  5.6 1.4 %collective-permute-done.10 = bf16[640,128]{1,0:T(8,128)(2,1)S(1)} collective-permute-done((bf16[640,128]{1,0:T(8,128)(2,1)S(1)}, bf16[640,128]{1,0:T(8,128)(2,1)S(1)}, u32[]{:S(2)}, u32[]{:S(2)}) %collective-permute-start.10) | collective-permute-done | bytes 163872 | tf_op jit(solution)/shard_map/ppermute | solution.py:317
  7.0 1.6 %collective-permute-start.11 = (bf16[320,128]{1,0:T(8,128)(2,1)S(1)}, bf16[320,128]{1,0:T(8,128)(2,1)S(1)}, u32[]{:S(2)}, u32[]{:S(2)}) collective-permute-start(bf16[320,128]{1,0:T(8,128)(2,1)S(1)} %fusion.1), channel_id=1, source_target_pairs={{0,16},{8,24},{16,0},{24,8},{1,17},{9,25},{17,1},{25,9},{2,18},{10... | collective-permute-start | bytes 245768 | tf_op jit(solution)/shard_map/ppermute | solution.py:318
  8.6 1.6 %collective-permute-start.1 = (bf16[248,512]{1,0:T(8,128)(2,1)}, bf16[248,512]{1,0:T(8,128)(2,1)S(1)}, u32[]{:S(2)}, u32[]{:S(2)}) collective-permute-start(bf16[248,512]{1,0:T(8,128)(2,1)} %get-tuple-element.17.refs_0_), channel_id=1, source_target_pairs={{2,0},{4,2},{6,4},{7,6},{5,7},{3,5},{1,3},{0,1},{10,8},{12,10},{14... | collective-permute-start | bytes 761864 | tf_op jit(solution)/shard_map/ppermute | solution.py:367
  10.2 4.1 %collective-permute-done.refs_1_ = bf16[248,512]{1,0:T(8,128)(2,1)S(1)} collective-permute-done((bf16[248,512]{1,0:T(8,128)(2,1)}, bf16[248,512]{1,0:T(8,128)(2,1)S(1)}, u32[]{:S(2)}, u32[]{:S(2)}) %collective-permute-start) | collective-permute-done | bytes 253984 | tf_op jit(solution)/shard_map/ppermute | solution.py:363
  14.3 0.3 collective-permute-start.2
  14.6 0.0 collective-permute-done.11
  14.7 1.9 %collective-permute-start.12 = (bf16[320,128]{1,0:T(8,128)(2,1)S(1)}, bf16[320,128]{1,0:T(8,128)(2,1)S(1)}, u32[]{:S(2)}, u32[]{:S(2)}) collective-permute-start(bf16[320,128]{1,0:T(8,128)(2,1)S(1)} %fusion), channel_id=1, source_target_pairs={{0,1},{1,0},{2,3},{3,2},{4,5},{5,4},{6,7},{7,6},{8,9},{9,8},{10,11... | collective-permute-start | bytes 245768 | tf_op jit(solution)/shard_map/ppermute | solution.py:319
  16.6 0.2 collective-permute-done.1.refs_2_
  16.7 1.6 %collective-permute-start.3 = (bf16[248,512]{1,0:T(8,128)(2,1)S(1)}, bf16[248,512]{1,0:T(8,128)(2,1)S(1)}, u32[]{:S(2)}, u32[]{:S(2)}) collective-permute-start(bf16[248,512]{1,0:T(8,128)(2,1)S(1)} %collective-permute-done.1.refs_2_), channel_id=1, source_target_pairs={{2,0},{4,2},{6,4},{7,6},{5,7},{3,5},{1,3},{0,1},{10,8},{12,10},{14... | collective-permute-start | bytes 761864 | tf_op jit(solution)/shard_map/ppermute | solution.py:367
  18.3 3.8 %collective-permute-done.2.refs_3_ = bf16[248,512]{1,0:T(8,128)(2,1)S(1)} collective-permute-done((bf16[248,512]{1,0:T(8,128)(2,1)S(1)}, bf16[248,512]{1,0:T(8,128)(2,1)S(1)}, u32[]{:S(2)}, u32[]{:S(2)}) %collective-permute-start.2) | collective-permute-done | bytes 253984 | tf_op jit(solution)/shard_map/ppermute | solution.py:363
  22.1 1.4 %collective-permute-start.4 = (bf16[248,512]{1,0:T(8,128)(2,1)S(1)}, bf16[248,512]{1,0:T(8,128)(2,1)S(1)}, u32[]{:S(2)}, u32[]{:S(2)}) collective-permute-start(bf16[248,512]{1,0:T(8,128)(2,1)S(1)} %collective-permute-done.2.refs_3_), channel_id=1, source_target_pairs={{0,2},{2,4},{4,6},{6,7},{7,5},{5,3},{3,1},{1,0},{8,10},{10,12},{12... | collective-permute-start | bytes 761864 | tf_op jit(solution)/shard_map/ppermute | solution.py:363
  23.5 0.0 collective-permute-done.12
  23.5 0.0 copy-start.8
  23.5 4.3 %collective-permute-start.15 = (bf16[320,128]{1,0:T(8,128)(2,1)S(1)}, bf16[320,128]{1,0:T(8,128)(2,1)S(1)}, u32[]{:S(2)}, u32[]{:S(2)}) collective-permute-start(bf16[320,128]{1,0:T(8,128)(2,1)S(1)} %add_convert_fusion.1), channel_id=1, source_target_pairs={{0,6},{1,7},{2,4},{3,5},{4,2},{5,3},{6,0},{7,1},{8,14},{9,15},{10,... | collective-permute-start | bytes 245768 | tf_op jit(solution)/shard_map/ppermute | solution.py:319
  27.8 0.0 collective-permute-start.14
  27.8 0.6 %collective-permute-start.13 = (bf16[320,128]{1,0:T(8,128)(2,1)S(1)}, bf16[320,128]{1,0:T(8,128)(2,1)S(1)}, u32[]{:S(2)}, u32[]{:S(2)}) collective-permute-start(bf16[320,128]{1,0:T(8,128)(2,1)S(1)} %add_convert_fusion.1), channel_id=1, source_target_pairs={{0,2},{1,3},{2,0},{3,1},{4,6},{5,7},{6,4},{7,5},{8,10},{9,11},{10,... | collective-permute-start | bytes 245768 | tf_op jit(solution)/shard_map/ppermute | solution.py:319
  28.5 0.0 collective-permute-done.3.refs_4_
  28.5 1.4 %collective-permute-start.5 = (bf16[248,512]{1,0:T(8,128)(2,1)S(1)}, bf16[248,512]{1,0:T(8,128)(2,1)S(1)}, u32[]{:S(2)}, u32[]{:S(2)}) collective-permute-start(bf16[248,512]{1,0:T(8,128)(2,1)S(1)} %collective-permute-done.3.refs_4_), channel_id=1, source_target_pairs={{2,0},{4,2},{6,4},{7,6},{5,7},{3,5},{1,3},{0,1},{10,8},{12,10},{14... | collective-permute-start | bytes 761864 | tf_op jit(solution)/shard_map/ppermute | solution.py:367
  29.9 0.3 collective-permute-done.4.refs_5_
  30.2 0.5 collective-permute-start.6
  30.7 4.7 %collective-permute-done.15 = bf16[320,128]{1,0:T(8,128)(2,1)S(1)} collective-permute-done((bf16[320,128]{1,0:T(8,128)(2,1)S(1)}, bf16[320,128]{1,0:T(8,128)(2,1)S(1)}, u32[]{:S(2)}, u32[]{:S(2)}) %collective-permute-start.15) | collective-permute-done | bytes 81952 | tf_op jit(solution)/shard_map/ppermute | solution.py:319
  35.4 3.8 %collective-permute-done.14 = bf16[320,128]{1,0:T(8,128)(2,1)S(1)} collective-permute-done((bf16[320,128]{1,0:T(8,128)(2,1)S(1)}, bf16[320,128]{1,0:T(8,128)(2,1)S(1)}, u32[]{:S(2)}, u32[]{:S(2)}) %collective-permute-start.14) | collective-permute-done | bytes 81952 | tf_op jit(solution)/shard_map/ppermute | solution.py:319
  39.2 0.0 collective-permute-done.13
  39.3 1.6 %collective-permute-start.16 = (bf16[320,128]{1,0:T(8,128)(2,1)S(1)}, bf16[320,128]{1,0:T(8,128)(2,1)S(1)}, u32[]{:S(2)}, u32[]{:S(2)}) collective-permute-start(bf16[320,128]{1,0:T(8,128)(2,1)S(1)} %add_convert_fusion.c0), channel_id=1, source_target_pairs={{0,16},{8,24},{16,0},{24,8},{1,17},{9,25},{17,1},{25,9},{2,18},{10... | collective-permute-start | bytes 245768 | tf_op jit(solution)/shard_map/ppermute | solution.py:318
  40.9 0.0 copy-done.8
  40.9 0.5 collective-permute-start.7
  41.4 0.0 collective-permute-start.17
  41.4 2.4 %collective-permute-done.16.c1 = bf16[320,128]{1,0:T(8,128)(2,1)S(1)} collective-permute-done((bf16[320,128]{1,0:T(8,128)(2,1)S(1)}, bf16[320,128]{1,0:T(8,128)(2,1)S(1)}, u32[]{:S(2)}, u32[]{:S(2)}) %collective-permute-start.16) | collective-permute-done | bytes 81952 | tf_op jit(solution)/shard_map/ppermute | solution.py:318
  43.8 0.0 collective-permute-start.18
  43.8 1.3 %collective-permute-done.7.refs_9_.p1 = bf16[256,128]{1,0:T(8,128)(2,1)S(1)} collective-permute-done((bf16[256,128]{1,0:T(8,128)(2,1)S(1)}, bf16[256,128]{1,0:T(8,128)(2,1)S(1)}, u32[]{:S(2)}, u32[]{:S(2)}) %collective-permute-start.7) | collective-permute-done | bytes 65568 | tf_op jit(solution)/shard_map/ppermute | solution.py:318
  45.1 0.0 collective-permute-start.8
  45.1 0.0 collective-permute-done.5.refs_6_
  45.1 0.5 collective-permute-start.9
  45.6 0.0 copy-done.2
  45.6 0.0 copy-done.1
  45.6 0.6 %prep.1 = (bf16[512,512]{1,0:T(8,128)(2,1)S(1)}, bf16[512,512]{1,0:T(8,128)(2,1)S(1)}, bf16[512,512]{1,0:T(8,128)(2,1)S(1)}, bf16[512,512]{1,0:T(8,128)(2,1)S(1)...) custom-call(f32[512,512]{1,0:T(8,128)S(1)} %copy-done.2, f32[512,512]{1,0:T(8,128)S(1)} %copy-done.1), custom_call_target="tpu_custom_call" | custom-call | flops 2621440 | bytes 4194304 | tf_op jit(solution)/shard_map/prep/pallas_call | solution.py:90
  46.3 0.0 collective-permute-done.6.refs_7_
  46.3 0.0 copy-done.3
  46.3 0.0 copy-done.4
  46.3 0.0 copy-start.9
  46.3 0.0 copy-start.10
  46.3 1.0 %crossing.1 = (f32[2,128,256]{2,1,0:T(8,128)S(1)}, bf16[2,128,256]{2,1,0:T(8,128)(2,1)S(1)}) custom-call(bf16[248,512]{1,0:T(8,128)(2,1)S(1)} %copy-done.4, bf16[248,512]{1,0:T(8,128)(2,1)S(1)} %collective-permute-done.refs_1_, bf16[248,512]{1,0:T(8,128)(2,1)S(1)} %collective-permute-done.1.refs_2_, bf16[248,512]{1,0:T(8,128)(2,1)S(1)} %collective-permute-done.2.refs_3_, ...), custom_call_target="tpu_custom_call" | custom-call | flops 520093696 | bytes 4194304 | tf_op jit(solution)/shard_map/crossing/pallas_call | solution.py:90
  47.3 0.1 collective-permute-start.19
  47.4 0.0 collective-permute-done.8.refs_10_.p2
  47.4 0.0 collective-permute-done.9.refs_11_.p3
  47.4 0.0 collective-permute-done.17.c2
  47.4 0.0 collective-permute-done.18.c3
  47.4 0.1 copy-done.9
  47.5 0.0 copy-done.10
  47.5 4.0 %solve.1 = (f32[512,512]{1,0:T(8,128)}, f32[128,256]{1,0:T(8,128)S(1)}) custom-call(bf16[320,128]{1,0:T(8,128)(2,1)S(1)} %add_convert_fusion.c0, bf16[320,128]{1,0:T(8,128)(2,1)S(1)} %collective-permute-done.16.c1, bf16[320,128]{1,0:T(8,128)(2,1)S(1)} %collective-permute-done.17.c2, bf16[320,128]{1,0:T(8,128)(2,1)S(1)} %collective-permute-done.18.c3, ...), custom_call_target="tpu_custom_call" | custom-call | flops 2415919104 | bytes 4194304 | tf_op jit(solution)/shard_map/solve/pallas_call | solution.py:90
  51.5 0.0 copy-done.5
  51.6 1.9 %below.1 = bf16[31,8,16,128]{3,2,1,0:T(8,128)(2,1)} custom-call(bf16[248,512]{1,0:T(8,128)(2,1)S(1)} %copy-done.4, bf16[248,512]{1,0:T(8,128)(2,1)S(1)} %collective-permute-done.refs_1_, bf16[248,512]{1,0:T(8,128)(2,1)S(1)} %collective-permute-done.1.refs_2_, bf16[248,512]{1,0:T(8,128)(2,1)S(1)} %collective-permute-done.2.refs_3_, ...), custom_call_target="tpu_custom_call" | custom-call | flops 520093696 | bytes 4194304 | tf_op jit(solution)/shard_map/below/pallas_call | solution.py:90
  53.5 0.0 collective-permute-done.19
  53.5 0.9 %collective-permute-start.20 = (bf16[128,256]{1,0:T(8,128)(2,1)S(1)}, bf16[128,256]{1,0:T(8,128)(2,1)S(1)}, u32[]{:S(2)}, u32[]{:S(2)}) collective-permute-start(bf16[128,256]{1,0:T(8,128)(2,1)S(1)} %fusion.2), channel_id=1, source_target_pairs={{0,16},{8,24},{16,0},{24,8},{1,17},{9,25},{17,1},{25,9},{2,18},{10... | collective-permute-start | bytes 196616 | tf_op jit(solution)/shard_map/ppermute | solution.py:318
  54.5 3.6 %collective-permute-done.20.recv = bf16[128,256]{1,0:T(8,128)(2,1)S(1)} collective-permute-done((bf16[128,256]{1,0:T(8,128)(2,1)S(1)}, bf16[128,256]{1,0:T(8,128)(2,1)S(1)}, u32[]{:S(2)}, u32[]{:S(2)}) %collective-permute-start.20) | collective-permute-done | bytes 65568 | tf_op jit(solution)/shard_map/ppermute | solution.py:318
  58.0 0.7 %prior_sum.1 = bf16[256,128]{1,0:T(8,128)(2,1)} custom-call(f32[128,256]{1,0:T(8,128)S(1)} %get-tuple-element.26.rest, f32[128,256]{1,0:T(8,128)S(1)} %dynamic-slice_bitcast_fusion.keep, bf16[128,256]{1,0:T(8,128)(2,1)S(1)} %collective-permute-done.20.recv), custom_call_target="tpu_custom_call" | custom-call | flops 327680 | bytes 262144 | tf_op jit(solution)/shard_map/prior_sum/pallas_call | solution.py:90
  (14 shorter events, 0.2 us)
Async XLA Ops:
  0.6 1.2 %copy-start = (f32[512,512]{1,0:T(8,128)S(1)}, f32[512,512]{1,0:T(8,128)}, u32[]{:S(2)}) copy-start(f32[512,512]{1,0:T(8,128)} %inv.3) | copy-start | bytes 3145732
  1.9 0.9 %copy-start.6 = (bf16[31,1,8,512]{3,2,1,0:T(8,128)(2,1)S(1)}, bf16[31,1,8,512]{3,2,1,0:T(8,128)(2,1)}, u32[]{:S(2)}) copy-start(bf16[31,1,8,512]{3,2,1,0:T(8,128)(2,1)} %param.15) | copy-start | bytes 761860
  2.8 0.9 %copy-start.7 = (bf16[31,1,8,512]{3,2,1,0:T(8,128)(2,1)S(1)}, bf16[31,1,8,512]{3,2,1,0:T(8,128)(2,1)}, u32[]{:S(2)}) copy-start(bf16[31,1,8,512]{3,2,1,0:T(8,128)(2,1)} %param.10) | copy-start | bytes 761860
  3.8 41.9 %copy-start.2 = (f32[512,512]{1,0:T(8,128)S(1)}, f32[512,512]{1,0:T(8,128)}, u32[]{:S(2)}) copy-start(f32[512,512]{1,0:T(8,128)} %fac.1) | copy-start | bytes 3145732
  5.6 40.1 %copy-start.1 = (f32[512,512]{1,0:T(8,128)S(1)}, f32[512,512]{1,0:T(8,128)}, u32[]{:S(2)}) copy-start(f32[512,512]{1,0:T(8,128)} %inv.3) | copy-start | bytes 3145732
  5.6 1.4 %collective-permute-start.10 = (bf16[640,128]{1,0:T(8,128)(2,1)S(1)}, bf16[640,128]{1,0:T(8,128)(2,1)S(1)}, u32[]{:S(2)}, u32[]{:S(2)}) collective-permute-start(bf16[640,128]{1,0:T(8,128)(2,1)S(1)} %get-tuple-element.19), channel_id=1, source_target_pairs={{0,8},{8,0},{16,24},{24,16},{1,9},{9,1},{17,25},{25,17},{2,10},{10... | collective-permute-start | bytes 491528 | tf_op jit(solution)/shard_map/ppermute | solution.py:317
  5.6 8.8 %collective-permute-start = (bf16[248,512]{1,0:T(8,128)(2,1)}, bf16[248,512]{1,0:T(8,128)(2,1)S(1)}, u32[]{:S(2)}, u32[]{:S(2)}) collective-permute-start(bf16[248,512]{1,0:T(8,128)(2,1)} %get-tuple-element.17.refs_0_), channel_id=1, source_target_pairs={{0,2},{2,4},{4,6},{6,7},{7,5},{5,3},{3,1},{1,0},{8,10},{10,12},{12... | collective-permute-start | bytes 761864 | tf_op jit(solution)/shard_map/ppermute | solution.py:363
  7.0 7.6 %collective-permute-start.11 = (bf16[320,128]{1,0:T(8,128)(2,1)S(1)}, bf16[320,128]{1,0:T(8,128)(2,1)S(1)}, u32[]{:S(2)}, u32[]{:S(2)}) collective-permute-start(bf16[320,128]{1,0:T(8,128)(2,1)S(1)} %fusion.1), channel_id=1, source_target_pairs={{0,16},{8,24},{16,0},{24,8},{1,17},{9,25},{17,1},{25,9},{2,18},{10... | collective-permute-start | bytes 245768 | tf_op jit(solution)/shard_map/ppermute | solution.py:318
  8.6 8.1 %collective-permute-start.1 = (bf16[248,512]{1,0:T(8,128)(2,1)}, bf16[248,512]{1,0:T(8,128)(2,1)S(1)}, u32[]{:S(2)}, u32[]{:S(2)}) collective-permute-start(bf16[248,512]{1,0:T(8,128)(2,1)} %get-tuple-element.17.refs_0_), channel_id=1, source_target_pairs={{2,0},{4,2},{6,4},{7,6},{5,7},{3,5},{1,3},{0,1},{10,8},{12,10},{14... | collective-permute-start | bytes 761864 | tf_op jit(solution)/shard_map/ppermute | solution.py:367
  14.3 7.8 %collective-permute-start.2 = (bf16[248,512]{1,0:T(8,128)(2,1)S(1)}, bf16[248,512]{1,0:T(8,128)(2,1)S(1)}, u32[]{:S(2)}, u32[]{:S(2)}) collective-permute-start(bf16[248,512]{1,0:T(8,128)(2,1)S(1)} %collective-permute-done.refs_1_), channel_id=1, source_target_pairs={{0,2},{2,4},{4,6},{6,7},{7,5},{5,3},{3,1},{1,0},{8,10},{10,12},{12... | collective-permute-start | bytes 761864 | tf_op jit(solution)/shard_map/ppermute | solution.py:363
  14.7 8.8 %collective-permute-start.12 = (bf16[320,128]{1,0:T(8,128)(2,1)S(1)}, bf16[320,128]{1,0:T(8,128)(2,1)S(1)}, u32[]{:S(2)}, u32[]{:S(2)}) collective-permute-start(bf16[320,128]{1,0:T(8,128)(2,1)S(1)} %fusion), channel_id=1, source_target_pairs={{0,1},{1,0},{2,3},{3,2},{4,5},{5,4},{6,7},{7,6},{8,9},{9,8},{10,11... | collective-permute-start | bytes 245768 | tf_op jit(solution)/shard_map/ppermute | solution.py:319
  16.7 11.7 %collective-permute-start.3 = (bf16[248,512]{1,0:T(8,128)(2,1)S(1)}, bf16[248,512]{1,0:T(8,128)(2,1)S(1)}, u32[]{:S(2)}, u32[]{:S(2)}) collective-permute-start(bf16[248,512]{1,0:T(8,128)(2,1)S(1)} %collective-permute-done.1.refs_2_), channel_id=1, source_target_pairs={{2,0},{4,2},{6,4},{7,6},{5,7},{3,5},{1,3},{0,1},{10,8},{12,10},{14... | collective-permute-start | bytes 761864 | tf_op jit(solution)/shard_map/ppermute | solution.py:367
  22.1 8.1 %collective-permute-start.4 = (bf16[248,512]{1,0:T(8,128)(2,1)S(1)}, bf16[248,512]{1,0:T(8,128)(2,1)S(1)}, u32[]{:S(2)}, u32[]{:S(2)}) collective-permute-start(bf16[248,512]{1,0:T(8,128)(2,1)S(1)} %collective-permute-done.2.refs_3_), channel_id=1, source_target_pairs={{0,2},{2,4},{4,6},{6,7},{7,5},{5,3},{3,1},{1,0},{8,10},{10,12},{12... | collective-permute-start | bytes 761864 | tf_op jit(solution)/shard_map/ppermute | solution.py:363
  23.5 17.4 %copy-start.8 = (bf16[128,2,1,128]{3,1,2,0:T(2,128)(2,1)S(1)}, bf16[128,2,1,128]{3,1,2,0:T(2,128)(2,1)}, u32[]{:S(2)}) copy-start(bf16[128,2,1,128]{3,1,2,0:T(2,128)(2,1)} %param.11) | copy-start | bytes 196612
  23.5 11.9 %collective-permute-start.15 = (bf16[320,128]{1,0:T(8,128)(2,1)S(1)}, bf16[320,128]{1,0:T(8,128)(2,1)S(1)}, u32[]{:S(2)}, u32[]{:S(2)}) collective-permute-start(bf16[320,128]{1,0:T(8,128)(2,1)S(1)} %add_convert_fusion.1), channel_id=1, source_target_pairs={{0,6},{1,7},{2,4},{3,5},{4,2},{5,3},{6,0},{7,1},{8,14},{9,15},{10,... | collective-permute-start | bytes 245768 | tf_op jit(solution)/shard_map/ppermute | solution.py:319
  27.8 11.4 %collective-permute-start.14 = (bf16[320,128]{1,0:T(8,128)(2,1)S(1)}, bf16[320,128]{1,0:T(8,128)(2,1)S(1)}, u32[]{:S(2)}, u32[]{:S(2)}) collective-permute-start(bf16[320,128]{1,0:T(8,128)(2,1)S(1)} %add_convert_fusion.1), channel_id=1, source_target_pairs={{0,4},{1,5},{2,6},{3,7},{4,0},{5,1},{6,2},{7,3},{8,12},{9,13},{10,... | collective-permute-start | bytes 245768 | tf_op jit(solution)/shard_map/ppermute | solution.py:319
  27.8 11.4 %collective-permute-start.13 = (bf16[320,128]{1,0:T(8,128)(2,1)S(1)}, bf16[320,128]{1,0:T(8,128)(2,1)S(1)}, u32[]{:S(2)}, u32[]{:S(2)}) collective-permute-start(bf16[320,128]{1,0:T(8,128)(2,1)S(1)} %add_convert_fusion.1), channel_id=1, source_target_pairs={{0,2},{1,3},{2,0},{3,1},{4,6},{5,7},{6,4},{7,5},{8,10},{9,11},{10,... | collective-permute-start | bytes 245768 | tf_op jit(solution)/shard_map/ppermute | solution.py:319
  28.5 16.7 %collective-permute-start.5 = (bf16[248,512]{1,0:T(8,128)(2,1)S(1)}, bf16[248,512]{1,0:T(8,128)(2,1)S(1)}, u32[]{:S(2)}, u32[]{:S(2)}) collective-permute-start(bf16[248,512]{1,0:T(8,128)(2,1)S(1)} %collective-permute-done.3.refs_4_), channel_id=1, source_target_pairs={{2,0},{4,2},{6,4},{7,6},{5,7},{3,5},{1,3},{0,1},{10,8},{12,10},{14... | collective-permute-start | bytes 761864 | tf_op jit(solution)/shard_map/ppermute | solution.py:367
  30.2 16.1 %collective-permute-start.6 = (bf16[248,512]{1,0:T(8,128)(2,1)S(1)}, bf16[248,512]{1,0:T(8,128)(2,1)S(1)}, u32[]{:S(2)}, u32[]{:S(2)}) collective-permute-start(bf16[248,512]{1,0:T(8,128)(2,1)S(1)} %collective-permute-done.4.refs_5_), channel_id=1, source_target_pairs={{0,2},{2,4},{4,6},{6,7},{7,5},{5,3},{3,1},{1,0},{8,10},{10,12},{12... | collective-permute-start | bytes 761864 | tf_op jit(solution)/shard_map/ppermute | solution.py:363
  39.3 4.5 %collective-permute-start.16 = (bf16[320,128]{1,0:T(8,128)(2,1)S(1)}, bf16[320,128]{1,0:T(8,128)(2,1)S(1)}, u32[]{:S(2)}, u32[]{:S(2)}) collective-permute-start(bf16[320,128]{1,0:T(8,128)(2,1)S(1)} %add_convert_fusion.c0), channel_id=1, source_target_pairs={{0,16},{8,24},{16,0},{24,8},{1,17},{9,25},{17,1},{25,9},{2,18},{10... | collective-permute-start | bytes 245768 | tf_op jit(solution)/shard_map/ppermute | solution.py:318
  40.9 5.4 %copy-start.3 = (bf16[31,1,64,2,1,128]{5,3,4,2,1,0:T(2,128)(2,1)S(1)}, bf16[31,1,64,2,1,128]{5,3,4,2,1,0:T(2,128)(2,1)}, u32[]{:S(2)}) copy-start(bf16[31,1,64,2,1,128]{5,3,4,2,1,0:T(2,128)(2,1)} %param.9) | copy-start | bytes 3047428
  40.9 5.4 %copy-start.4 = (bf16[248,512]{1,0:T(8,128)(2,1)S(1)}, bf16[248,512]{1,0:T(8,128)(2,1)}, u32[]{:S(2)}) copy-start(bf16[248,512]{1,0:T(8,128)(2,1)} %get-tuple-element.17.refs_0_) | copy-start | bytes 761860
  40.9 4.3 %collective-permute-start.7 = (bf16[256,128]{1,0:T(8,128)(2,1)S(1)}, bf16[256,128]{1,0:T(8,128)(2,1)S(1)}, u32[]{:S(2)}, u32[]{:S(2)}) collective-permute-start(bf16[256,128]{1,0:T(8,128)(2,1)S(1)} %bitcast.31), channel_id=1, source_target_pairs={{0,16},{8,24},{16,0},{24,8},{1,17},{9,25},{17,1},{25,9},{2,18},{10... | collective-permute-start | bytes 196616 | tf_op jit(solution)/shard_map/ppermute | solution.py:318
  41.4 6.1 %collective-permute-start.17 = (bf16[320,128]{1,0:T(8,128)(2,1)S(1)}, bf16[320,128]{1,0:T(8,128)(2,1)S(1)}, u32[]{:S(2)}, u32[]{:S(2)}) collective-permute-start(bf16[320,128]{1,0:T(8,128)(2,1)S(1)} %add_convert_fusion.c0), channel_id=1, source_target_pairs={{0,8},{8,0},{16,24},{24,16},{1,9},{9,1},{17,25},{25,17},{2,10},{10... | collective-permute-start | bytes 245768 | tf_op jit(solution)/shard_map/ppermute | solution.py:317
  43.8 3.7 %collective-permute-start.18 = (bf16[320,128]{1,0:T(8,128)(2,1)S(1)}, bf16[320,128]{1,0:T(8,128)(2,1)S(1)}, u32[]{:S(2)}, u32[]{:S(2)}) collective-permute-start(bf16[320,128]{1,0:T(8,128)(2,1)S(1)} %collective-permute-done.16.c1), channel_id=1, source_target_pairs={{0,8},{8,0},{16,24},{24,16},{1,9},{9,1},{17,25},{25,17},{2,10},{10... | collective-permute-start | bytes 245768 | tf_op jit(solution)/shard_map/ppermute | solution.py:317
  45.1 2.3 %collective-permute-start.8 = (bf16[256,128]{1,0:T(8,128)(2,1)S(1)}, bf16[256,128]{1,0:T(8,128)(2,1)S(1)}, u32[]{:S(2)}, u32[]{:S(2)}) collective-permute-start(bf16[256,128]{1,0:T(8,128)(2,1)S(1)} %bitcast.32), channel_id=1, source_target_pairs={{0,8},{8,0},{16,24},{24,16},{1,9},{9,1},{17,25},{25,17},{2,10},{10... | collective-permute-start | bytes 196616 | tf_op jit(solution)/shard_map/ppermute | solution.py:317
  45.1 2.3 %collective-permute-start.9 = (bf16[256,128]{1,0:T(8,128)(2,1)S(1)}, bf16[256,128]{1,0:T(8,128)(2,1)S(1)}, u32[]{:S(2)}, u32[]{:S(2)}) collective-permute-start(bf16[256,128]{1,0:T(8,128)(2,1)S(1)} %collective-permute-done.7.refs_9_.p1), channel_id=1, source_target_pairs={{0,8},{8,0},{16,24},{24,16},{1,9},{9,1},{17,25},{25,17},{2,10},{10... | collective-permute-start | bytes 196616 | tf_op jit(solution)/shard_map/ppermute | solution.py:317
  46.3 1.2 %copy-start.9 = (f32[512,512]{1,0:T(8,128)S(1)}, f32[512,512]{1,0:T(8,128)}, u32[]{:S(2)}) copy-start(f32[512,512]{1,0:T(8,128)} %dadj.1) | copy-start | bytes 3145732
  46.3 1.2 %copy-start.10 = (bf16[128,2,1,128]{3,1,2,0:T(2,128)(2,1)S(1)}, bf16[128,2,1,128]{3,1,2,0:T(2,128)(2,1)}, u32[]{:S(2)}) copy-start(bf16[128,2,1,128]{3,1,2,0:T(2,128)(2,1)} %param.16) | copy-start | bytes 196612
  47.3 6.2 %collective-permute-start.19 = (bf16[2,128,256]{2,1,0:T(8,128)(2,1)S(1)}, bf16[2,128,256]{2,1,0:T(8,128)(2,1)S(1)}, u32[]{:S(2)}, u32[]{:S(2)}) collective-permute-start(bf16[2,128,256]{2,1,0:T(8,128)(2,1)S(1)} %get-tuple-element.28), channel_id=1, source_target_pairs={{0,8},{8,0},{16,24},{24,16},{1,9},{9,1},{17,25},{25,17},{2,10},{10... | collective-permute-start | bytes 393224 | tf_op jit(solution)/shard_map/ppermute | solution.py:317
  47.5 4.0 %copy-start.5 = (bf16[31,1,64,2,1,128]{5,3,4,2,1,0:T(2,128)(2,1)S(1)}, bf16[31,1,64,2,1,128]{5,3,4,2,1,0:T(2,128)(2,1)}, u32[]{:S(2)}) copy-start(bf16[31,1,64,2,1,128]{5,3,4,2,1,0:T(2,128)(2,1)} %param.14) | copy-start | bytes 3047428
  53.5 4.5 %collective-permute-start.20 = (bf16[128,256]{1,0:T(8,128)(2,1)S(1)}, bf16[128,256]{1,0:T(8,128)(2,1)S(1)}, u32[]{:S(2)}, u32[]{:S(2)}) collective-permute-start(bf16[128,256]{1,0:T(8,128)(2,1)S(1)} %fusion.2), channel_id=1, source_target_pairs={{0,16},{8,24},{16,0},{24,8},{1,17},{9,25},{17,1},{25,9},{2,18},{10... | collective-permute-start | bytes 196616 | tf_op jit(solution)/shard_map/ppermute | solution.py:318

commit v2 on v1

v2 whole, which is shorter than its diff:
```python
import functools

import jax
import jax.numpy as jnp
from jax import lax
from jax.experimental import pallas as pl
from jax.experimental.pallas import tpu as pltpu
from jax.sharding import PartitionSpec as P

BF = jnp.bfloat16
F32 = jnp.float32
BLK = 128


def row_product(left_rows, right_rows):
    return lax.dot_general(
        left_rows, right_rows, (((0,), (0,)), ((), ())), preferred_element_type=F32
    )


def diag_solve(diag_factor, diag_inverse, diag_reduced):
    highest = lax.Precision.HIGHEST
    chol_proj = jnp.dot(diag_factor.T, diag_reduced, precision=highest)
    phi_lower = jnp.tril(chol_proj) - 0.5 * jnp.diag(jnp.diagonal(chol_proj))
    symmetric = 0.5 * (phi_lower + phi_lower.T)
    left_side = jnp.dot(diag_inverse.T, symmetric, precision=highest)
    return jnp.dot(left_side, diag_inverse, precision=highest)


def local_any(
    below_factor,
    panel_factor,
    prior_factor,
    diag_factor,
    diag_inverse,
    below_adjoint,
    panel_adjoint,
    prior_adjoint,
    diag_adjoint,
):
    tile_count = below_factor.shape[0]
    tile_rows = below_factor.shape[2]
    local_rows = tile_count * tile_rows
    local_cols = below_factor.shape[3] * below_factor.shape[5]
    own_rows = panel_factor.shape[2]
    width = panel_factor.shape[3]
    prior_local = prior_factor.shape[0]
    below_mat = below_factor.reshape(local_rows, local_cols)
    below_bar = below_adjoint.reshape(local_rows, local_cols)
    inverse_bf = diag_inverse.astype(BF)
    own_grad = jnp.dot(
        panel_adjoint.reshape(tile_count * own_rows, width),
        inverse_bf,
        preferred_element_type=F32,
    ).astype(BF)
    summed = lax.psum(
        row_product(own_grad, panel_factor.reshape(tile_count * own_rows, width)).astype(BF),
        ("gr", "gc"),
    ).astype(F32)
    panel_grad = own_grad.reshape(panel_adjoint.shape)
    grad_rows = lax.all_gather(panel_grad, "gc", axis=2, tiled=True).reshape(local_rows, width)
    diag_reduced = jnp.tril(diag_adjoint - summed)
    diag_gradient = diag_solve(diag_factor, diag_inverse, diag_reduced)
    prior_here = prior_factor.reshape(prior_local, local_cols)
    prior_whole = lax.all_gather(prior_here, "gr", axis=0, tiled=True)
    below_new = (
        below_bar.astype(F32) - jnp.dot(grad_rows, prior_whole, preferred_element_type=F32)
    ).astype(BF)
    crossing = lax.psum_scatter(
        row_product(grad_rows, below_mat).astype(BF), "gr", scatter_dimension=0, tiled=True
    ).astype(F32)
    twice_rows = lax.dynamic_slice_in_dim(
        2.0 * diag_gradient, lax.axis_index("gr") * prior_local, prior_local, 0
    ).astype(BF)
    curvature = jnp.dot(twice_rows, prior_whole, preferred_element_type=F32)
    prior_bar = prior_adjoint.reshape(prior_local, local_cols).astype(F32)
    prior_new = (prior_bar - crossing - curvature).astype(BF)
    return (
        below_new.reshape(below_adjoint.shape),
        panel_grad,
        prior_new.reshape(prior_adjoint.shape),
        diag_gradient,
    )


TIES = {'r1': 'sum', 'r2': 'none', 'r3': 'z1sum', 'r4': 'none', 's1': 'z1', 's2': 'z1', 's3': 'z2sum', 's4': 'none', 'pf': 'xsum', 'prep': 'xsum', 'below': 'ag'}
SPLIT, CUT, LATE, LIM = True, 112, False, 40 * 2**20
VM = pl.BlockSpec(memory_space=pltpu.VMEM)
ANYM = pl.BlockSpec(memory_space=pl.ANY)


def call(body, outs, ins, scratch=(), flops=0, nbytes=0, name=None, specs=None,
         out_specs=None, limit=LIM, alias=None):
    return pl.pallas_call(
        body,
        out_shape=[jax.ShapeDtypeStruct(s, d) for s, d in outs],
        in_specs=specs or [VM] * len(ins),
        out_specs=out_specs or [VM] * len(outs),
        scratch_shapes=list(scratch),
        compiler_params=pltpu.CompilerParams(vmem_limit_bytes=limit),
        cost_estimate=pl.CostEstimate(flops=flops, bytes_accessed=nbytes, transcendentals=0),
        name=name,
        input_output_aliases=alias or {},
    )(*ins)


def lower_blocks(count):
    return [(r, c) for r in range(count) for c in range(r + 1)]


def my_core():
    return lax.rem(lax.axis_index("gr"), 2)


def my_y():
    return lax.div(lax.axis_index("gr"), 2)


def grad_kernel(adj, fac, inv, prior, grad, keep, send, adj_v, fac_v, inv_v, grad_v, sems):
    half = keep.shape[0]
    pairs = [(adj, adj_v), (inv, inv_v), (fac, fac_v), (prior, send.at[half:, :])]
    copies = [
        pltpu.make_async_copy(src, dst, sems.at[k]) for k, (src, dst) in enumerate(pairs)
    ]
    for copy in copies:
        copy.start()
    copies[0].wait()
    copies[1].wait()
    grad_v[...] = jnp.dot(
        adj_v[...], inv_v[...].astype(BF), preferred_element_type=F32
    ).astype(BF)
    back = pltpu.make_async_copy(grad_v, grad, sems.at[4])
    back.start()
    copies[2].wait()
    blocks = lower_blocks(adj.shape[1] // BLK)
    core = my_core()
    whole = row_product(grad_v[...], fac_v[...])
    for at, (row, col) in enumerate(blocks):
        which, place = divmod(at * BLK, half)
        piece = whole[row * BLK : (row + 1) * BLK, col * BLK : (col + 1) * BLK]
        here = pl.ds(place, BLK)

        @pl.when(core == which)
        def _():
            keep[here, :] = piece

        @pl.when(core != which)
        def _():
            send[here, :] = piece.astype(BF)

    copies[3].wait()
    back.wait()


def split(value):
    high = value.astype(BF)
    return high, (value - high.astype(F32)).astype(BF)


def prep_kernel(fac, inv, fac_t_hi, fac_t_lo, inv_t_hi, inv_t_lo, inv_hi, inv_lo, done):
    done[...] = jnp.zeros_like(done)
    fac_t_hi[...], fac_t_lo[...] = split(fac[...].T)
    inverse = inv[...]
    inv_t_hi[...], inv_t_lo[...] = split(inverse.T)
    inv_hi[...], inv_lo[...] = split(inverse)


def dot2(a_hi, a_lo, b):
    d = functools.partial(jnp.dot, preferred_element_type=F32)
    return d(a_hi, b) + d(a_lo, b)


def dot2r(a, b_hi, b_lo):
    d = functools.partial(jnp.dot, preferred_element_type=F32)
    return d(a, b_hi) + d(a, b_lo)


def natural(view, scratch):
    rows = view.shape[0] // 2
    scratch[...] = view.astype(F32)
    return jnp.concatenate(
        [scratch[pl.ds(t, rows, stride=2), :] for t in range(2)], axis=1
    ).astype(BF)


def natural_prior(own, other, scratch, whole):
    rows = own.shape[0] // 2
    core, y = my_core(), my_y()
    for ref, where in ((own, y), (other, 1 - y)):
        for k in range(2):
            at = pl.multiple_of((2 * where + jnp.bitwise_xor(core, k)) * BLK, BLK)
            whole[pl.ds(at, BLK), :] = natural(ref[k * rows : (k + 1) * rows, :], scratch)


def solve_kernel(
    c_own, c_y, c_core, prior, bar, dadj,
    fac_t_hi, fac_t_lo, inv_t_hi, inv_t_lo, inv_hi, inv_lo, *others
):
    out, rest, cross, full, twice, inter = others[-6:]
    quarter = c_own.shape[0]
    core, y = my_core(), my_y()
    for where, off, ref in ((core, y, c_own[...]), (core, 1 - y, c_y[...]),
                            (1 - core, y, c_core[:quarter, :]),
                            (1 - core, 1 - y, c_core[quarter:, :])):
        at = pl.multiple_of((2 * where + off) * quarter, quarter)
        cross[pl.ds(at, quarter), :] = ref.astype(F32)
    size = dadj.shape[0]
    half = size // 2
    blocks = lower_blocks(size // BLK)
    top, low = slice(0, half), slice(half, size)
    r_at = lax.broadcasted_iota(jnp.int32, (half, half), 0)
    c_at = lax.broadcasted_iota(jnp.int32, (half, half), 1)

    def reduced(rows, cols):
        strips = []
        for row in range(rows.start // BLK, rows.stop // BLK):
            parts = []
            for col in range(cols.start // BLK, cols.stop // BLK):
                if col > row:
                    parts.append(jnp.zeros((BLK, BLK), F32))
                    continue
                at = blocks.index((row, col))
                here = dadj[row * BLK : (row + 1) * BLK, col * BLK : (col + 1) * BLK]
                parts.append(here - cross[at * BLK : (at + 1) * BLK, :])
            strips.append(jnp.concatenate(parts, axis=1))
        return jnp.concatenate(strips, axis=0)

    def lower(value, scale):
        zero = jnp.zeros_like(value)
        return jnp.where(r_at > c_at, value, jnp.where(r_at == c_at, scale * value, zero))

    d_tt = lower(reduced(top, top), 1.0).astype(BF)
    d_lt = reduced(low, top).astype(BF)
    d_ll = lower(reduced(low, low), 1.0).astype(BF)
    p_tt = dot2(fac_t_hi[top, :], fac_t_lo[top, :], jnp.concatenate([d_tt, d_lt], axis=0))
    p_l = dot2(
        fac_t_hi[low, low], fac_t_lo[low, low], jnp.concatenate([d_lt, d_ll], axis=1)
    )
    f_tt = lower(p_tt, 0.5).astype(BF)
    f_lt = p_l[:, top].astype(BF)
    f_ll = lower(p_l[:, low], 0.5).astype(BF)
    a_tt = dot2(inv_t_hi[top, :], inv_t_lo[top, :], jnp.concatenate([f_tt, f_lt], axis=0))
    a_tl = dot2(inv_t_hi[top, low], inv_t_lo[top, low], f_ll)
    a_l = dot2(
        inv_t_hi[low, low], inv_t_lo[low, low], jnp.concatenate([f_lt, f_ll], axis=1)
    )
    left = jnp.concatenate(
        [
            jnp.concatenate([a_tt, a_tl], axis=1).astype(BF),
            a_l.astype(BF),
        ],
        axis=0,
    )
    full[:, top] = dot2r(left, inv_hi[:, top], inv_lo[:, top])
    full[:, low] = dot2r(left[:, low], inv_hi[low, low], inv_lo[low, low])
    value = full[...]
    grad = 0.5 * (value + value.T)
    out[...] = grad
    twice[...] = 2.0 * grad
    own = pl.multiple_of(lax.axis_index("gr") * BLK, BLK)
    rows = twice[pl.ds(own, BLK), :].astype(BF)
    curvature = jnp.dot(rows, prior[...], preferred_element_type=F32)
    inter[...] = bar[...].astype(F32)
    prior_bar = jnp.concatenate(
        [inter[pl.ds(t, BLK, stride=2), :] for t in range(2)], axis=1
    )
    rest[...] = prior_bar - curvature


def final_kernel(rest, keep, recv, out, inter):
    value = rest[...] - (keep[...] + recv[...].astype(F32))
    for t in range(2):
        inter[pl.ds(t, BLK, stride=2), :] = value[:, t * BLK : (t + 1) * BLK]
    out[...] = inter[...].astype(BF)


def ring_order(n):
    return list(range(0, n, 2)) + list(range(n - 1, 0, -2))


def shard_of(offset, n):
    me = lax.axis_index("gc")
    half = lax.div(me, 2)
    pos = jnp.where(lax.rem(me, 2) == 0, half, n - 1 - half)
    at = lax.rem(pos - offset + 2 * n, n)
    return jnp.where(at < n // 2, 2 * at, 2 * (n - 1 - at) + 1)


def accumulate(grad, off, n, below, inter, acc, first):
    j = shard_of(off, n)
    view = below[:, j]
    rows = natural(view.reshape(view.shape[0] * view.shape[1], view.shape[2]), inter)
    part = row_product(grad[...], rows)
    if first:
        acc[...] = part
    else:
        acc[...] += part


def step_kernel(offsets, n, first, *refs):
    if first:
        own, *parts, inv, below, acc = refs[: len(offsets) + 4]
        grads, inter = refs[len(offsets) + 4 : -1], refs[-1]
        accumulate(own, 0, n, below, inter, acc, True)
    else:
        *parts, inv, below, before, acc = refs[: len(offsets) + 4]
        grads, inter = refs[len(offsets) + 4 : -1], refs[-1]
        acc[...] = before[...]
    inverse = inv[...].astype(BF)
    for off, part, grad in zip(offsets, parts, grads):
        grad[...] = jnp.dot(part[...], inverse, preferred_element_type=F32).astype(BF)
        accumulate(grad, off, n, below, inter, acc, False)


def last_kernel(offset, n, count, *refs):
    parts = refs[:count]
    inv, below, before, keep, send, grad, inter, acc = refs[count:]
    acc[...] = before[...]
    inverse = inv[...].astype(BF)
    at = 0
    for part in parts:
        grad[at : at + part.shape[0], :] = jnp.dot(
            part[...], inverse, preferred_element_type=F32
        ).astype(BF)
        at += part.shape[0]
    accumulate(grad, offset, n, below, inter, acc, False)
    core = my_core()
    for which in range(2):
        for y in range(2):
            piece = acc[(2 * y + which) * BLK : (2 * y + which + 1) * BLK, :]

            @pl.when(core == which)
            def _():
                keep[y] = piece

            @pl.when(core != which)
            def _():
                send[y] = piece.astype(BF)


def spread(prod, inter):
    for t in range(2):
        inter[pl.ds(t, prod.shape[0], stride=2), :] = prod[:, t * BLK : (t + 1) * BLK]


def below_kernel(offsets, n, *refs):
    grads = refs[: len(offsets)]
    p_own, p_other, bar, out, last, whole, done, inter, small = refs[len(offsets) :]
    done[...] = jnp.zeros_like(done)
    natural_prior(p_own, p_other, small, whole)
    for grad, off in zip(grads, offsets):
        j = shard_of(off, n)
        spread(jnp.dot(grad[...], whole[...], preferred_element_type=F32), inter)
        view = bar[:, j]
        old = view.reshape(view.shape[0] * view.shape[1], view.shape[2]).astype(F32)
        out[:, j] = (old - inter[...]).astype(BF).reshape(view.shape)
    rest = bar[:, shard_of(n // 2, n)]
    last[...] = rest.reshape(rest.shape[0] * rest.shape[1], rest.shape[2])


def below_last_kernel(n, early, grad, whole, bar, out, inter, block, sem):
    spread(jnp.dot(grad[...], whole[...], preferred_element_type=F32), inter)
    block[...] = (bar[...].astype(F32) - inter[...]).astype(BF).reshape(block.shape)
    copy = pltpu.make_async_copy(block, out.at[:, shard_of(n // 2, n)], sem)
    copy.start()
    copy.wait()


def in_hbm(value):
    return pltpu.with_memory_space_constraint(value, pltpu.HBM)


def tie(value, *after):
    return lax.optimization_barrier((value, *after))[0]


def xor_perm(n, bit):
    return [(i, i ^ bit) for i in range(n)]


def local_fast(
    below_factor,
    panel_factor,
    prior_factor,
    diag_factor,
    diag_inverse,
    below_adjoint,
    panel_adjoint,
    prior_adjoint,
    diag_adjoint,
    n_gr,
    n_gc,
):
    tiles, _, tile_rows, ct, _, cb = below_factor.shape
    own_rows, width = panel_factor.shape[2:]
    shard_rows = tiles * own_rows
    cols = ct * cb
    prior_local = prior_factor.shape[0]
    core = lambda v: lax.ppermute(v, "gr", xor_perm(n_gr, 1))
    ynb = lambda v: lax.ppermute(v, "gr", xor_perm(n_gr, 2))
    gcx = lambda v, bit: lax.ppermute(v, "gc", xor_perm(n_gc, bit))
    cyc = ring_order(n_gc)
    right = [(cyc[i], cyc[(i + 1) % n_gc]) for i in range(n_gc)]
    left = [(b, a) for a, b in right]

    bf_view = below_factor.reshape(tiles, n_gc, own_rows * ct, cb)
    ba_view = below_adjoint.reshape(tiles, n_gc, own_rows * ct, cb)
    pf_view = prior_factor.reshape(prior_local * ct, cb)
    pa_view = prior_adjoint.reshape(prior_local * ct, cb)

    n_blocks = len(lower_blocks(width // BLK))
    half_rows = n_blocks // 2 * BLK
    quarter = half_rows // 2
    adj2 = panel_adjoint.reshape(shard_rows, width)
    shard = ((shard_rows, width), BF)
    token = ((8, BLK), F32)

    def step_call(name, offs, parts, acc=None):
        return call(
            functools.partial(step_kernel, offs, n_gc, acc is None),
            [((width, cols), F32)] + [shard] * len(offs),
            [*parts, diag_inverse, bf_view] + ([] if acc is None else [acc]),
            scratch=[pltpu.VMEM((shard_rows * ct, cb), F32)],
            name=name,
        )

    grad, keep, send = call(
        grad_kernel,
        [
            ((shard_rows, width), BF),
            ((half_rows, BLK), F32),
            ((half_rows + prior_local * ct, BLK), BF),
        ],
        [
            in_hbm(v)
            for v in (adj2, panel_factor.reshape(shard_rows, width), diag_inverse, pf_view)
        ],
        scratch=[
            pltpu.VMEM((shard_rows, width), BF),
            pltpu.VMEM((shard_rows, width), BF),
            pltpu.VMEM((width, width), F32),
            pltpu.VMEM((shard_rows, width), BF),
            pltpu.SemaphoreType.DMA((5,)),
        ],
        name="panel_grad",
        specs=[ANYM] * 4,
        out_specs=[ANYM, VM, VM],
    )

    to_right = lambda v: lax.ppermute(v, "gc", right)
    to_left = lambda v: lax.ppermute(v, "gc", left)
    plus = lambda a, b: (a.astype(F32) + b.astype(F32)).astype(BF)
    y = my_y()
    env = {}
    done = {}

    def need(item):
        if item in done:
            return
        done[item] = True
        if item == "r1":
            env["r1"] = [to_right(adj2), to_left(adj2)]
        elif item in ("r2", "r3"):
            before = "r%d" % (int(item[1]) - 1)
            need(before)
            u, v = env[before]
            env[item] = [to_right(u), to_left(v)]
        elif item == "r4":
            need("r3")
            u, v = env["r3"]
            env[item] = [to_right(u[:CUT]), to_left(v[CUT:])] if SPLIT else [to_right(u)]
        elif item in ("s1", "s2", "s3"):
            k = int(item[1])
            need("r%d" % k)
            if k > 1:
                need("s%d" % (k - 1))
            lead = [grad] if k == 1 else []
            acc, *out = step_call(
                "step_%d" % k, [k, -k], [*lead, *env["r%d" % k]],
                None if k == 1 else env["s%d" % (k - 1)][0],
            )
            env[item], env["g%d" % k] = [acc], out
        elif item == "prep":
            *out, mark = call(
                prep_kernel,
                [((width, width), BF)] * 6 + [token],
                [diag_factor, diag_inverse],
                name="prep",
            )
            env["prepared"], env[item] = out, [mark]
        elif item == "pf":
            env[item] = [ynb(env["pair"])]
        elif item == "below":
            need("s3")
            need("pf")
            offsets = [0, 1, -1, 2, -2, 3, -3]
            grads = [grad, *env["g1"], *env["g2"], *env["g3"]]
            out, bar, whole, mark = call(
                functools.partial(below_kernel, offsets, n_gc),
                [(ba_view.shape, BF), ((shard_rows * ct, cb), BF), ((width, cols), BF), token],
                [*grads, env["pair"], *env["pf"], ba_view],
                scratch=[
                    pltpu.VMEM((shard_rows * ct, cb), F32),
                    pltpu.VMEM((prior_local * ct, cb), F32),
                ],
                name="below_early",
            )
            env["early"], env[item] = (out, bar, whole), [mark]
        elif item == "s4":
            need("r4")
            need("s3")
            keep_x, send_x, g4 = call(
                functools.partial(last_kernel, n_gc // 2, n_gc, len(env["r4"])),
                [((2, BLK, cols), F32), ((2, BLK, cols), BF), ((shard_rows, width), BF)],
                [*env["r4"], diag_inverse, bf_view, env["s3"][0]],
                scratch=[
                    pltpu.VMEM((shard_rows * ct, cb), F32),
                    pltpu.VMEM((width, cols), F32),
                ],
                name="step_four",
            )
            both_x = keep_x + core(send_x).astype(F32)
            env["mine_x"] = lax.dynamic_index_in_dim(both_x, y, 0, keepdims=False)
            other_x = lax.dynamic_index_in_dim(both_x, 1 - y, 0, keepdims=False).astype(BF)
            env["g4"], env[item] = g4, [other_x]

    def gate(point, value):
        items = [k for k, v in TIES.items() if v == point]
        for item in items:
            need(item)
        vals = [v for item in items for v in env[item]]
        if not vals:
            return value
        value, *vals = lax.optimization_barrier((value, *vals))
        for item in items:
            env[item] = [vals.pop(0) for _ in env[item]]
        return value

    got = gate("sum", core(gate("core", send)))
    both = (keep + got[:half_rows].astype(F32)).reshape(2, quarter, BLK)
    mine = lax.dynamic_index_in_dim(both, y, 0, keepdims=False)
    other = lax.dynamic_index_in_dim(both, 1 - y, 0, keepdims=False).astype(BF)
    env["pair"] = jnp.concatenate([pf_view, got[half_rows:]], axis=0)
    part = plus(mine, gate("ysum", ynb(gate("y", other))))
    for k, name in enumerate(("x", "z1", "z2")):
        part = gate(name, part)
        part = plus(part, gate(name + "sum", gcx(part, 1 << k)))
    part = gate("ag", part)
    part_y = gate("agsum", ynb(part))
    part_c = core(jnp.concatenate([part, part_y], axis=0))
    for item in ("prep", "below", "s4"):
        need(item)
    got_x = ynb(env["s4"][0])
    prepared = env["prepared"]
    below_early, last_bar, prior_whole = env["early"]
    marks = env["prep"] + env["below"]
    g4 = env["g4"]
    if LATE:
        part_c = tie(part_c, env["s4"][0])

    diag_gradient, rest = call(
        solve_kernel,
        [((width, width), F32), ((prior_local, cols), F32)],
        [part, part_y, part_c, prior_whole, pa_view, diag_adjoint, *prepared, *marks],
        scratch=[
            pltpu.VMEM((n_blocks * BLK, BLK), F32),
            pltpu.VMEM((width, width), F32),
            pltpu.VMEM((width, width), F32),
            pltpu.VMEM((prior_local * ct, cb), F32),
        ],
        flops=18 * width**3,
        nbytes=2**22,
        name="solve",
        specs=[VM] * 12 + [ANYM] * len(marks),
    )
    (below_new,) = call(
        functools.partial(below_last_kernel, n_gc),
        [(ba_view.shape, BF)],
        [below_early, g4, prior_whole, last_bar],
        scratch=[
            pltpu.VMEM((shard_rows * ct, cb), F32),
            pltpu.VMEM((tiles, own_rows * ct, cb), BF),
            pltpu.SemaphoreType.DMA(()),
        ],
        name="below_last",
        specs=[ANYM] + [VM] * 3,
        out_specs=[ANYM],
        alias={0: 0},
    )
    (prior_new,) = call(
        final_kernel,
        [(pa_view.shape, BF)],
        [rest, env["mine_x"], got_x],
        scratch=[pltpu.VMEM((prior_local * ct, cb), F32)],
        flops=10 * prior_local * cols,
        nbytes=2**18,
        name="prior_sum",
    )
    return (
        below_new.reshape(below_adjoint.shape),
        grad.reshape(panel_adjoint.shape),
        prior_new.reshape(prior_adjoint.shape),
        diag_gradient,
    )


def solution(mesh):
    n_gr, n_gc = mesh.shape["gr"], mesh.shape["gc"]

    def local(*args):
        below_factor, panel_factor, prior_factor = args[:3]
        fits = (
            n_gr == 4
            and n_gc == 8
            and panel_factor.shape[2] == 8
            and below_factor.shape[3] == 2
            and below_factor.shape[5] == BLK
            and prior_factor.shape[0] == BLK
        )
        if fits:
            return local_fast(*args, n_gr=n_gr, n_gc=n_gc)
        return local_any(*args)

    in_specs = (
        P(None, "gr", None, None, "gc", None),
        P(None, "gr", "gc", None),
        P("gr", None, "gc", None),
        P(),
        P(),
        P(None, "gr", None, None, "gc", None),
        P(None, "gr", "gc", None),
        P("gr", None, "gc", None),
        P(),
    )
    out_specs = (
        P(None, "gr", None, None, "gc", None),
        P(None, "gr", "gc", None),
        P("gr", None, "gc", None),
        P(),
    )
    return jax.shard_map(local, mesh=mesh, in_specs=in_specs, out_specs=out_specs, check_vma=False)
```

time: 58.9 us -> 48.6 us (0.83)
  the two profiles are of different devices: /device:TPU:2 before, /device:TPU:0 now
where the time goes in v2:
time: 48.6 us; the launch traced here: 48.4 us
  starting transfers between devices  20.2 us (42%)
  waiting for transfers between devices  14.1 us (29%)
  Pallas kernels  13 us (27%)
  between operations  0.91 us (2%)
    pallas_call x10, Pallas kernels, call(): pl.pallas_call(body, out_shape=[jax.ShapeDtypeStruct(s, d) for s, d in ou...  13 us
    ppermute x3, waiting for transfers between devices, local_fast(): gcx = lambda v, bit: lax.ppermute(v, 'gc', xor_perm(n_gc, bit))  6.47 us
    ppermute x4, starting transfers between devices, local_fast(): ynb = lambda v: lax.ppermute(v, 'gr', xor_perm(n_gr, 2))  5.4 us
    ppermute x3, starting transfers between devices, local_fast(): gcx = lambda v, bit: lax.ppermute(v, 'gc', xor_perm(n_gc, bit))  4.85 us
    ppermute x4, starting transfers between devices, local_fast(): to_right = lambda v: lax.ppermute(v, 'gc', right)  4.82 us
    ppermute x4, starting transfers between devices, local_fast(): to_left = lambda v: lax.ppermute(v, 'gc', left)  4.39 us
    ppermute x4, waiting for transfers between devices, local_fast(): to_right = lambda v: lax.ppermute(v, 'gc', right)  4.01 us
    ppermute x4, waiting for transfers between devices, local_fast(): to_left = lambda v: lax.ppermute(v, 'gc', left)  1.55 us
  transfers between devices with their start and end apart: 18, of which 9 were waited for; matrix products, arithmetic and copies ran while one was open for 0% of the time, Pallas kernels for 25%

profile of v2, /device:TPU:0, one launch (start us, length us, event | category | flops | bytes accessed | tf_op | source)
XLA Modules:
  0.0 48.4 jit_solution(10912053621346454033)
XLA Ops:
  0.6 3.1 %collective-permute-start.1 = (bf16[248,512]{1,0:T(8,128)(2,1)}, bf16[248,512]{1,0:T(8,128)(2,1)S(1)}, u32[]{:S(2)}, u32[]{:S(2)}) collective-permute-start(bf16[248,512]{1,0:T(8,128)(2,1)} %bitcast.39), channel_id=1, source_target_pairs={{0,2},{2,4},{4,6},{6,7},{7,5},{5,3},{3,1},{1,0},{8,10},{10,12},{12... | collective-permute-start | bytes 761864 | tf_op jit(solution)/shard_map/ppermute | solution.py:450
  3.7 0.0 collective-permute-start.2
  3.7 0.0 copy-start.2
  3.7 2.5 %panel_grad.1 = (bf16[248,512]{1,0:T(8,128)(2,1)}, f32[640,128]{1,0:T(8,128)S(1)}, bf16[896,128]{1,0:T(8,128)(2,1)S(1)}) custom-call(bf16[248,512]{1,0:T(8,128)(2,1)} %bitcast.41, bf16[248,512]{1,0:T(8,128)(2,1)} %bitcast.38, f32[512,512]{1,0:T(8,128)} %refs_2_.5, bf16[256,128]{1,0:T(8,128)(2,1)} %bitcast.36), custom_call_target="tpu_custom_call" | custom-call | tf_op jit(solution)/shard_map/panel_grad/pallas_call | solution.py:94
  6.2 0.0 copy-start
  6.2 0.1 collective-permute-start
  6.3 1.5 %collective-permute-done = bf16[896,128]{1,0:T(8,128)(2,1)S(1)} collective-permute-done((bf16[896,128]{1,0:T(8,128)(2,1)S(1)}, bf16[896,128]{1,0:T(8,128)(2,1)S(1)}, u32[]{:S(2)}, u32[]{:S(2)}) %collective-permute-start) | collective-permute-done | bytes 229408 | tf_op jit(solution)/shard_map/ppermute | solution.py:399
  7.8 2.2 %collective-permute-done.1.refs_1_ = bf16[248,512]{1,0:T(8,128)(2,1)S(1)} collective-permute-done((bf16[248,512]{1,0:T(8,128)(2,1)}, bf16[248,512]{1,0:T(8,128)(2,1)S(1)}, u32[]{:S(2)}, u32[]{:S(2)}) %collective-permute-start.1) | collective-permute-done | bytes 253984 | tf_op jit(solution)/shard_map/ppermute | solution.py:450
  10.0 1.5 %collective-permute-done.2.refs_2_ = bf16[248,512]{1,0:T(8,128)(2,1)S(1)} collective-permute-done((bf16[248,512]{1,0:T(8,128)(2,1)}, bf16[248,512]{1,0:T(8,128)(2,1)S(1)}, u32[]{:S(2)}, u32[]{:S(2)}) %collective-permute-start.2) | collective-permute-done | bytes 253984 | tf_op jit(solution)/shard_map/ppermute | solution.py:451
  11.5 0.0 copy-start.7
  11.6 1.6 %collective-permute-start.5 = (bf16[320,128]{1,0:T(8,128)(2,1)S(1)}, bf16[320,128]{1,0:T(8,128)(2,1)S(1)}, u32[]{:S(2)}, u32[]{:S(2)}) collective-permute-start(bf16[320,128]{1,0:T(8,128)(2,1)S(1)} %fusion.1), channel_id=1, source_target_pairs={{0,16},{8,24},{16,0},{24,8},{1,17},{9,25},{17,1},{25,9},{2,18},{10... | collective-permute-start | bytes 245768 | tf_op jit(solution)/shard_map/ppermute | solution.py:400
  13.2 0.0 copy-done.7
  13.2 0.8 %collective-permute-start.7 = (bf16[512,128]{1,0:T(8,128)(2,1)S(1)}, bf16[512,128]{1,0:T(8,128)(2,1)S(1)}, u32[]{:S(2)}, u32[]{:S(2)}) collective-permute-start(bf16[512,128]{1,0:T(8,128)(2,1)S(1)} %pad_maximum_fusion.1.refs_7_), channel_id=1, source_target_pairs={{0,16},{8,24},{16,0},{24,8},{1,17},{9,25},{17,1},{25,9},{2,18},{10... | collective-permute-start | bytes 393224 | tf_op jit(solution)/shard_map/ppermute | solution.py:400
  14.0 1.6 %collective-permute-start.3 = (bf16[248,512]{1,0:T(8,128)(2,1)S(1)}, bf16[248,512]{1,0:T(8,128)(2,1)S(1)}, u32[]{:S(2)}, u32[]{:S(2)}) collective-permute-start(bf16[248,512]{1,0:T(8,128)(2,1)S(1)} %collective-permute-done.1.refs_1_), channel_id=1, source_target_pairs={{0,2},{2,4},{4,6},{6,7},{7,5},{5,3},{3,1},{1,0},{8,10},{10,12},{12... | collective-permute-start | bytes 761864 | tf_op jit(solution)/shard_map/ppermute | solution.py:450
  15.6 0.4 collective-permute-start.4
  16.0 0.5 collective-permute-done.5
  16.5 0.0 copy-start.1
  16.5 0.0 copy-start.4
  16.5 0.6 %collective-permute-start.6 = (bf16[320,128]{1,0:T(8,128)(2,1)S(1)}, bf16[320,128]{1,0:T(8,128)(2,1)S(1)}, u32[]{:S(2)}, u32[]{:S(2)}) collective-permute-start(bf16[320,128]{1,0:T(8,128)(2,1)S(1)} %fusion), channel_id=1, source_target_pairs={{0,1},{1,0},{2,3},{3,2},{4,5},{5,4},{6,7},{7,6},{8,9},{9,8},{10,11... | collective-permute-start | bytes 245768 | tf_op jit(solution)/shard_map/ppermute | solution.py:401
  17.1 0.0 copy-done.2
  17.1 0.0 copy-done
  17.1 0.6 %prep.1 = (bf16[512,512]{1,0:T(8,128)(2,1)S(1)}, bf16[512,512]{1,0:T(8,128)(2,1)S(1)}, bf16[512,512]{1,0:T(8,128)(2,1)S(1)}, bf16[512,512]{1,0:T(8,128)(2,1)S(1)...) custom-call(f32[512,512]{1,0:T(8,128)S(1)} %copy-done.2, f32[512,512]{1,0:T(8,128)S(1)} %copy-done), custom_call_target="tpu_custom_call" | custom-call | tf_op jit(solution)/shard_map/prep/pallas_call | solution.py:94
  17.8 0.0 copy-done.1
  17.8 0.0 copy-done.4
  17.8 0.9 %step_1.1 = (f32[512,256]{1,0:T(8,128)S(1)}, bf16[248,512]{1,0:T(8,128)(2,1)S(1)}, bf16[248,512]{1,0:T(8,128)(2,1)S(1)}) custom-call(bf16[248,512]{1,0:T(8,128)(2,1)S(1)} %copy-done.4, bf16[248,512]{1,0:T(8,128)(2,1)S(1)} %collective-permute-done.1.refs_1_, bf16[248,512]{1,0:T(8,128)(2,1)S(1)} %collective-permute-done.2.refs_2_, f32[512,512]{1,0:T(8,128)S(1)} %copy-done, ...), custom_call_target="tpu_custom_call" | custom-call | tf_op jit(solution)/shard_map/step_1/pallas_call | solution.py:94
  18.7 0.0 collective-permute-done.7.refs_8_
  18.7 3.4 %collective-permute-done.6 = bf16[320,128]{1,0:T(8,128)(2,1)S(1)} collective-permute-done((bf16[320,128]{1,0:T(8,128)(2,1)S(1)}, bf16[320,128]{1,0:T(8,128)(2,1)S(1)}, u32[]{:S(2)}, u32[]{:S(2)}) %collective-permute-start.6) | collective-permute-done | bytes 81952 | tf_op jit(solution)/shard_map/ppermute | solution.py:401
  22.1 0.0 collective-permute-done.4.refs_1_
  22.1 1.9 %collective-permute-start.10 = (bf16[248,512]{1,0:T(8,128)(2,1)S(1)}, bf16[248,512]{1,0:T(8,128)(2,1)S(1)}, u32[]{:S(2)}, u32[]{:S(2)}) collective-permute-start(bf16[248,512]{1,0:T(8,128)(2,1)S(1)} %collective-permute-done.4.refs_1_), channel_id=1, source_target_pairs={{2,0},{4,2},{6,4},{7,6},{5,7},{3,5},{1,3},{0,1},{10,8},{12,10},{14... | collective-permute-start | bytes 761864 | tf_op jit(solution)/shard_map/ppermute | solution.py:451
  24.1 0.0 collective-permute-done.3.refs_0_
  24.1 0.1 collective-permute-start.9
  24.2 1.0 %step_2.1 = (f32[512,256]{1,0:T(8,128)S(1)}, bf16[248,512]{1,0:T(8,128)(2,1)S(1)}, bf16[248,512]{1,0:T(8,128)(2,1)S(1)}) custom-call(bf16[248,512]{1,0:T(8,128)(2,1)S(1)} %collective-permute-done.3.refs_0_, bf16[248,512]{1,0:T(8,128)(2,1)S(1)} %collective-permute-done.4.refs_1_, f32[512,512]{1,0:T(8,128)S(1)} %copy-done, ...), custom_call_target="tpu_custom_call" | custom-call | tf_op jit(solution)/shard_map/step_2/pallas_call | solution.py:94
  25.3 1.5 %collective-permute-start.8 = (bf16[320,128]{1,0:T(8,128)(2,1)S(1)}, bf16[320,128]{1,0:T(8,128)(2,1)S(1)}, u32[]{:S(2)}, u32[]{:S(2)}) collective-permute-start(bf16[320,128]{1,0:T(8,128)(2,1)S(1)} %add_convert_fusion.2), channel_id=1, source_target_pairs={{0,2},{1,3},{2,0},{3,1},{4,6},{5,7},{6,4},{7,5},{8,10},{9,11},{10,... | collective-permute-start | bytes 245768 | tf_op jit(solution)/shard_map/ppermute | solution.py:401
  26.7 3.0 %collective-permute-done.8 = bf16[320,128]{1,0:T(8,128)(2,1)S(1)} collective-permute-done((bf16[320,128]{1,0:T(8,128)(2,1)S(1)}, bf16[320,128]{1,0:T(8,128)(2,1)S(1)}, u32[]{:S(2)}, u32[]{:S(2)}) %collective-permute-start.8) | collective-permute-done | bytes 81952 | tf_op jit(solution)/shard_map/ppermute | solution.py:401
  29.8 0.0 collective-permute-done.10.refs_1_
  29.8 0.6 %collective-permute-done.9.refs_0_ = bf16[248,512]{1,0:T(8,128)(2,1)S(1)} collective-permute-done((bf16[248,512]{1,0:T(8,128)(2,1)S(1)}, bf16[248,512]{1,0:T(8,128)(2,1)S(1)}, u32[]{:S(2)}, u32[]{:S(2)}) %collective-permute-start.9) | collective-permute-done | bytes 253984 | tf_op jit(solution)/shard_map/ppermute | solution.py:450
  30.4 2.8 %collective-permute-start.13 = (bf16[320,128]{1,0:T(8,128)(2,1)S(1)}, bf16[320,128]{1,0:T(8,128)(2,1)S(1)}, u32[]{:S(2)}, u32[]{:S(2)}) collective-permute-start(bf16[320,128]{1,0:T(8,128)(2,1)S(1)} %add_convert_fusion.1), channel_id=1, source_target_pairs={{0,4},{1,5},{2,6},{3,7},{4,0},{5,1},{6,2},{7,3},{8,12},{9,13},{10,... | collective-permute-start | bytes 245768 | tf_op jit(solution)/shard_map/ppermute | solution.py:401
  33.2 0.0 copy-start.3
  33.2 1.0 %step_3.1 = (f32[512,256]{1,0:T(8,128)S(1)}, bf16[248,512]{1,0:T(8,128)(2,1)S(1)}, bf16[248,512]{1,0:T(8,128)(2,1)S(1)}) custom-call(bf16[248,512]{1,0:T(8,128)(2,1)S(1)} %collective-permute-done.9.refs_0_, bf16[248,512]{1,0:T(8,128)(2,1)S(1)} %collective-permute-done.10.refs_1_, f32[512,512]{1,0:T(8,128)S(1)} %copy-done, ...), custom_call_target="tpu_custom_call" | custom-call | tf_op jit(solution)/shard_map/step_3/pallas_call | solution.py:94
  34.3 2.0 %collective-permute-start.12 = (bf16[136,512]{1,0:T(8,128)(2,1)S(1)}, bf16[136,512]{1,0:T(8,128)(2,1)S(1)}, u32[]{:S(2)}, u32[]{:S(2)}) collective-permute-start(bf16[136,512]{1,0:T(8,128)(2,1)S(1)} %slice.15), channel_id=1, source_target_pairs={{2,0},{4,2},{6,4},{7,6},{5,7},{3,5},{1,3},{0,1},{10,8},{12,10},{14... | collective-permute-start | bytes 417800 | tf_op jit(solution)/shard_map/ppermute | solution.py:451
  36.3 0.1 collective-permute-start.11
  36.4 0.0 copy-done.3
  36.4 1.8 %below_early.1 = (bf16[31,8,16,128]{3,2,1,0:T(8,128)(2,1)}, bf16[496,128]{1,0:T(8,128)(2,1)S(1)}, bf16[512,256]{1,0:T(8,128)(2,1)S(1)}, f32[8,128]{1,0:T(8,128)S(1)}) custom-call(bf16[248,512]{1,0:T(8,128)(2,1)S(1)} %copy-done.4, bf16[248,512]{1,0:T(8,128)(2,1)S(1)} %get-tuple-element.51.refs_1_, bf16[248,512]{1,0:T(8,128)(2,1)S(1)} %get-tuple-element.52.refs_2_, ...), custom_call_target="tpu_custom_call" | custom-call | tf_op jit(solution)/shard_map/below_early/pallas_call | solution.py:94
  38.2 0.0 collective-permute-done.13
  38.2 1.6 %collective-permute-start.14 = (bf16[320,128]{1,0:T(8,128)(2,1)S(1)}, bf16[320,128]{1,0:T(8,128)(2,1)S(1)}, u32[]{:S(2)}, u32[]{:S(2)}) collective-permute-start(bf16[320,128]{1,0:T(8,128)(2,1)S(1)} %add_convert_fusion.c_own), channel_id=1, source_target_pairs={{0,16},{8,24},{16,0},{24,8},{1,17},{9,25},{17,1},{25,9},{2,18},{10... | collective-permute-start | bytes 245768 | tf_op jit(solution)/shard_map/ppermute | solution.py:400
  39.9 1.2 %collective-permute-done.11.refs_0_ = bf16[112,512]{1,0:T(8,128)(2,1)S(1)} collective-permute-done((bf16[112,512]{1,0:T(8,128)(2,1)S(1)}, bf16[112,512]{1,0:T(8,128)(2,1)S(1)}, u32[]{:S(2)}, u32[]{:S(2)}) %collective-permute-start.11) | collective-permute-done | bytes 114720 | tf_op jit(solution)/shard_map/ppermute | solution.py:450
  41.1 0.0 collective-permute-done.12.refs_1_
  41.1 0.6 %step_four.1 = (f32[2,128,256]{2,1,0:T(8,128)S(1)}, bf16[2,128,256]{2,1,0:T(8,128)(2,1)S(1)}, bf16[248,512]{1,0:T(8,128)(2,1)S(1)}) custom-call(bf16[112,512]{1,0:T(8,128)(2,1)S(1)} %collective-permute-done.11.refs_0_, bf16[136,512]{1,0:T(8,128)(2,1)S(1)} %collective-permute-done.12.refs_1_, f32[512,512]{1,0:T(8,128)S(1)} %copy-done, ...), custom_call_target="tpu_custom_call" | custom-call | tf_op jit(solution)/shard_map/step_four/pallas_call | solution.py:94
  41.7 0.1 collective-permute-start.16
  41.8 0.9 %below_last.1 = bf16[31,8,16,128]{3,2,1,0:T(8,128)(2,1)} custom-call(bf16[31,8,16,128]{3,2,1,0:T(8,128)(2,1)} %get-tuple-element.68.early, bf16[248,512]{1,0:T(8,128)(2,1)S(1)} %get-tuple-element.72.grad, bf16[512,256]{1,0:T(8,128)(2,1)S(1)} %get-tuple-element.73.whole.prior, bf16[496,128]{1,0:T(8,128)(2,1)S(1)} %get-tuple-element.74.bar), custom_call_target="tpu_custom_call", output_to_operand_aliasing={{}: (0, {})} | custom-call | tf_op jit(solution)/shard_map/below_last/pallas_call | solution.py:94
  42.7 0.0 copy-start.5
  42.8 0.0 collective-permute-done.14.c_y
  42.8 0.6 %collective-permute-start.15 = (bf16[640,128]{1,0:T(8,128)(2,1)S(1)}, bf16[640,128]{1,0:T(8,128)(2,1)S(1)}, u32[]{:S(2)}, u32[]{:S(2)}) collective-permute-start(bf16[640,128]{1,0:T(8,128)(2,1)S(1)} %pad_maximum_fusion), channel_id=1, source_target_pairs={{0,8},{8,0},{16,24},{24,16},{1,9},{9,1},{17,25},{25,17},{2,10},{10... | collective-permute-start | bytes 491528 | tf_op jit(solution)/shard_map/ppermute | solution.py:399
  43.3 0.0 collective-permute-done.16
  43.4 0.0 copy-start.6
  43.4 1.4 %collective-permute-start.17 = (bf16[128,256]{1,0:T(8,128)(2,1)S(1)}, bf16[128,256]{1,0:T(8,128)(2,1)S(1)}, u32[]{:S(2)}, u32[]{:S(2)}) collective-permute-start(bf16[128,256]{1,0:T(8,128)(2,1)S(1)} %fusion.2), channel_id=1, source_target_pairs={{0,16},{8,24},{16,0},{24,8},{1,17},{9,25},{17,1},{25,9},{2,18},{10... | collective-permute-start | bytes 196616 | tf_op jit(solution)/shard_map/ppermute | solution.py:400
  44.8 0.0 collective-permute-done.15.c_core
  44.8 0.0 copy-done.5
  44.8 0.0 copy-done.6
  44.8 2.8 %solve.1 = (f32[512,512]{1,0:T(8,128)}, f32[128,256]{1,0:T(8,128)S(1)}) custom-call(bf16[320,128]{1,0:T(8,128)(2,1)S(1)} %add_convert_fusion.c_own, bf16[320,128]{1,0:T(8,128)(2,1)S(1)} %collective-permute-done.14.c_y, bf16[640,128]{1,0:T(8,128)(2,1)S(1)} %collective-permute-done.15.c_core, bf16[512,256]{1,0:T(8,128)(2,1)S(1)} %get-tuple-element.73.whole.prior, ...), custom_call_target="tpu_custom_call" | custom-call | flops 2415919104 | bytes 4194304 | tf_op jit(solution)/shard_map/solve/pallas_call | solution.py:94
  47.6 0.1 collective-permute-done.17.recv
  47.7 0.7 %prior_sum.1 = bf16[256,128]{1,0:T(8,128)(2,1)} custom-call(f32[128,256]{1,0:T(8,128)S(1)} %get-tuple-element.86.rest, f32[128,256]{1,0:T(8,128)S(1)} %dynamic-slice_bitcast_fusion.keep, bf16[128,256]{1,0:T(8,128)(2,1)S(1)} %collective-permute-done.17.recv), custom_call_target="tpu_custom_call" | custom-call | flops 327680 | bytes 262144 | tf_op jit(solution)/shard_map/prior_sum/pallas_call | solution.py:94
  (14 shorter events, 0.2 us)
Async XLA Ops:
  0.6 9.3 %collective-permute-start.1 = (bf16[248,512]{1,0:T(8,128)(2,1)}, bf16[248,512]{1,0:T(8,128)(2,1)S(1)}, u32[]{:S(2)}, u32[]{:S(2)}) collective-permute-start(bf16[248,512]{1,0:T(8,128)(2,1)} %bitcast.39), channel_id=1, source_target_pairs={{0,2},{2,4},{4,6},{6,7},{7,5},{5,3},{3,1},{1,0},{8,10},{10,12},{12... | collective-permute-start | bytes 761864 | tf_op jit(solution)/shard_map/ppermute | solution.py:450
  3.7 7.8 %collective-permute-start.2 = (bf16[248,512]{1,0:T(8,128)(2,1)}, bf16[248,512]{1,0:T(8,128)(2,1)S(1)}, u32[]{:S(2)}, u32[]{:S(2)}) collective-permute-start(bf16[248,512]{1,0:T(8,128)(2,1)} %bitcast.40), channel_id=1, source_target_pairs={{2,0},{4,2},{6,4},{7,6},{5,7},{3,5},{1,3},{0,1},{10,8},{12,10},{14... | collective-permute-start | bytes 761864 | tf_op jit(solution)/shard_map/ppermute | solution.py:451
  3.7 13.4 %copy-start.2 = (f32[512,512]{1,0:T(8,128)S(1)}, f32[512,512]{1,0:T(8,128)}, u32[]{:S(2)}) copy-start(f32[512,512]{1,0:T(8,128)} %fac.1) | copy-start | bytes 3145732
  6.2 10.9 %copy-start = (f32[512,512]{1,0:T(8,128)S(1)}, f32[512,512]{1,0:T(8,128)}, u32[]{:S(2)}) copy-start(f32[512,512]{1,0:T(8,128)} %refs_2_.5) | copy-start | bytes 3145732
  6.2 1.6 %collective-permute-start = (bf16[896,128]{1,0:T(8,128)(2,1)S(1)}, bf16[896,128]{1,0:T(8,128)(2,1)S(1)}, u32[]{:S(2)}, u32[]{:S(2)}) collective-permute-start(bf16[896,128]{1,0:T(8,128)(2,1)S(1)} %get-tuple-element.48), channel_id=1, source_target_pairs={{0,8},{8,0},{16,24},{24,16},{1,9},{9,1},{17,25},{25,17},{2,10},{10... | collective-permute-start | bytes 688136 | tf_op jit(solution)/shard_map/ppermute | solution.py:399
  11.5 1.6 %copy-start.7 = (bf16[128,2,1,128]{3,1,2,0:T(2,128)(2,1)S(1)}, bf16[128,2,1,128]{3,1,2,0:T(2,128)(2,1)}, u32[]{:S(2)}) copy-start(bf16[128,2,1,128]{3,1,2,0:T(2,128)(2,1)} %param.11) | copy-start | bytes 196612
  11.6 4.9 %collective-permute-start.5 = (bf16[320,128]{1,0:T(8,128)(2,1)S(1)}, bf16[320,128]{1,0:T(8,128)(2,1)S(1)}, u32[]{:S(2)}, u32[]{:S(2)}) collective-permute-start(bf16[320,128]{1,0:T(8,128)(2,1)S(1)} %fusion.1), channel_id=1, source_target_pairs={{0,16},{8,24},{16,0},{24,8},{1,17},{9,25},{17,1},{25,9},{2,18},{10... | collective-permute-start | bytes 245768 | tf_op jit(solution)/shard_map/ppermute | solution.py:400
  13.2 5.5 %collective-permute-start.7 = (bf16[512,128]{1,0:T(8,128)(2,1)S(1)}, bf16[512,128]{1,0:T(8,128)(2,1)S(1)}, u32[]{:S(2)}, u32[]{:S(2)}) collective-permute-start(bf16[512,128]{1,0:T(8,128)(2,1)S(1)} %pad_maximum_fusion.1.refs_7_), channel_id=1, source_target_pairs={{0,16},{8,24},{16,0},{24,8},{1,17},{9,25},{17,1},{25,9},{2,18},{10... | collective-permute-start | bytes 393224 | tf_op jit(solution)/shard_map/ppermute | solution.py:400
  14.0 10.1 %collective-permute-start.3 = (bf16[248,512]{1,0:T(8,128)(2,1)S(1)}, bf16[248,512]{1,0:T(8,128)(2,1)S(1)}, u32[]{:S(2)}, u32[]{:S(2)}) collective-permute-start(bf16[248,512]{1,0:T(8,128)(2,1)S(1)} %collective-permute-done.1.refs_1_), channel_id=1, source_target_pairs={{0,2},{2,4},{4,6},{6,7},{7,5},{5,3},{3,1},{1,0},{8,10},{10,12},{12... | collective-permute-start | bytes 761864 | tf_op jit(solution)/shard_map/ppermute | solution.py:450
  15.6 6.6 %collective-permute-start.4 = (bf16[248,512]{1,0:T(8,128)(2,1)S(1)}, bf16[248,512]{1,0:T(8,128)(2,1)S(1)}, u32[]{:S(2)}, u32[]{:S(2)}) collective-permute-start(bf16[248,512]{1,0:T(8,128)(2,1)S(1)} %collective-permute-done.2.refs_2_), channel_id=1, source_target_pairs={{2,0},{4,2},{6,4},{7,6},{5,7},{3,5},{1,3},{0,1},{10,8},{12,10},{14... | collective-permute-start | bytes 761864 | tf_op jit(solution)/shard_map/ppermute | solution.py:451
  16.5 1.2 %copy-start.1 = (bf16[31,1,64,2,1,128]{5,3,4,2,1,0:T(2,128)(2,1)S(1)}, bf16[31,1,64,2,1,128]{5,3,4,2,1,0:T(2,128)(2,1)}, u32[]{:S(2)}) copy-start(bf16[31,1,64,2,1,128]{5,3,4,2,1,0:T(2,128)(2,1)} %param.9) | copy-start | bytes 3047428
  16.5 1.2 %copy-start.4 = (bf16[248,512]{1,0:T(8,128)(2,1)S(1)}, bf16[248,512]{1,0:T(8,128)(2,1)}, u32[]{:S(2)}) copy-start(bf16[248,512]{1,0:T(8,128)(2,1)} %get-tuple-element.47.refs_0_) | copy-start | bytes 761860
  16.5 5.6 %collective-permute-start.6 = (bf16[320,128]{1,0:T(8,128)(2,1)S(1)}, bf16[320,128]{1,0:T(8,128)(2,1)S(1)}, u32[]{:S(2)}, u32[]{:S(2)}) collective-permute-start(bf16[320,128]{1,0:T(8,128)(2,1)S(1)} %fusion), channel_id=1, source_target_pairs={{0,1},{1,0},{2,3},{3,2},{4,5},{5,4},{6,7},{7,6},{8,9},{9,8},{10,11... | collective-permute-start | bytes 245768 | tf_op jit(solution)/shard_map/ppermute | solution.py:401
  22.1 7.6 %collective-permute-start.10 = (bf16[248,512]{1,0:T(8,128)(2,1)S(1)}, bf16[248,512]{1,0:T(8,128)(2,1)S(1)}, u32[]{:S(2)}, u32[]{:S(2)}) collective-permute-start(bf16[248,512]{1,0:T(8,128)(2,1)S(1)} %collective-permute-done.4.refs_1_), channel_id=1, source_target_pairs={{2,0},{4,2},{6,4},{7,6},{5,7},{3,5},{1,3},{0,1},{10,8},{12,10},{14... | collective-permute-start | bytes 761864 | tf_op jit(solution)/shard_map/ppermute | solution.py:451
  24.1 6.3 %collective-permute-start.9 = (bf16[248,512]{1,0:T(8,128)(2,1)S(1)}, bf16[248,512]{1,0:T(8,128)(2,1)S(1)}, u32[]{:S(2)}, u32[]{:S(2)}) collective-permute-start(bf16[248,512]{1,0:T(8,128)(2,1)S(1)} %collective-permute-done.3.refs_0_), channel_id=1, source_target_pairs={{0,2},{2,4},{4,6},{6,7},{7,5},{5,3},{3,1},{1,0},{8,10},{10,12},{12... | collective-permute-start | bytes 761864 | tf_op jit(solution)/shard_map/ppermute | solution.py:450
  25.3 4.5 %collective-permute-start.8 = (bf16[320,128]{1,0:T(8,128)(2,1)S(1)}, bf16[320,128]{1,0:T(8,128)(2,1)S(1)}, u32[]{:S(2)}, u32[]{:S(2)}) collective-permute-start(bf16[320,128]{1,0:T(8,128)(2,1)S(1)} %add_convert_fusion.2), channel_id=1, source_target_pairs={{0,2},{1,3},{2,0},{3,1},{4,6},{5,7},{6,4},{7,5},{8,10},{9,11},{10,... | collective-permute-start | bytes 245768 | tf_op jit(solution)/shard_map/ppermute | solution.py:401
  30.4 7.8 %collective-permute-start.13 = (bf16[320,128]{1,0:T(8,128)(2,1)S(1)}, bf16[320,128]{1,0:T(8,128)(2,1)S(1)}, u32[]{:S(2)}, u32[]{:S(2)}) collective-permute-start(bf16[320,128]{1,0:T(8,128)(2,1)S(1)} %add_convert_fusion.1), channel_id=1, source_target_pairs={{0,4},{1,5},{2,6},{3,7},{4,0},{5,1},{6,2},{7,3},{8,12},{9,13},{10,... | collective-permute-start | bytes 245768 | tf_op jit(solution)/shard_map/ppermute | solution.py:401
  33.2 3.1 %copy-start.3 = (bf16[31,1,64,2,1,128]{5,3,4,2,1,0:T(2,128)(2,1)S(1)}, bf16[31,1,64,2,1,128]{5,3,4,2,1,0:T(2,128)(2,1)}, u32[]{:S(2)}) copy-start(bf16[31,1,64,2,1,128]{5,3,4,2,1,0:T(2,128)(2,1)} %param.14) | copy-start | bytes 3047428
  34.3 6.8 %collective-permute-start.12 = (bf16[136,512]{1,0:T(8,128)(2,1)S(1)}, bf16[136,512]{1,0:T(8,128)(2,1)S(1)}, u32[]{:S(2)}, u32[]{:S(2)}) collective-permute-start(bf16[136,512]{1,0:T(8,128)(2,1)S(1)} %slice.15), channel_id=1, source_target_pairs={{2,0},{4,2},{6,4},{7,6},{5,7},{3,5},{1,3},{0,1},{10,8},{12,10},{14... | collective-permute-start | bytes 417800 | tf_op jit(solution)/shard_map/ppermute | solution.py:451
  36.3 4.8 %collective-permute-start.11 = (bf16[112,512]{1,0:T(8,128)(2,1)S(1)}, bf16[112,512]{1,0:T(8,128)(2,1)S(1)}, u32[]{:S(2)}, u32[]{:S(2)}) collective-permute-start(bf16[112,512]{1,0:T(8,128)(2,1)S(1)} %slice.14), channel_id=1, source_target_pairs={{0,2},{2,4},{4,6},{6,7},{7,5},{5,3},{3,1},{1,0},{8,10},{10,12},{12... | collective-permute-start | bytes 344072 | tf_op jit(solution)/shard_map/ppermute | solution.py:450
  38.2 4.5 %collective-permute-start.14 = (bf16[320,128]{1,0:T(8,128)(2,1)S(1)}, bf16[320,128]{1,0:T(8,128)(2,1)S(1)}, u32[]{:S(2)}, u32[]{:S(2)}) collective-permute-start(bf16[320,128]{1,0:T(8,128)(2,1)S(1)} %add_convert_fusion.c_own), channel_id=1, source_target_pairs={{0,16},{8,24},{16,0},{24,8},{1,17},{9,25},{17,1},{25,9},{2,18},{10... | collective-permute-start | bytes 245768 | tf_op jit(solution)/shard_map/ppermute | solution.py:400
  41.7 1.6 %collective-permute-start.16 = (bf16[2,128,256]{2,1,0:T(8,128)(2,1)S(1)}, bf16[2,128,256]{2,1,0:T(8,128)(2,1)S(1)}, u32[]{:S(2)}, u32[]{:S(2)}) collective-permute-start(bf16[2,128,256]{2,1,0:T(8,128)(2,1)S(1)} %get-tuple-element.88), channel_id=1, source_target_pairs={{0,8},{8,0},{16,24},{24,16},{1,9},{9,1},{17,25},{25,17},{2,10},{10... | collective-permute-start | bytes 393224 | tf_op jit(solution)/shard_map/ppermute | solution.py:399
  42.7 2.1 %copy-start.5 = (f32[512,512]{1,0:T(8,128)S(1)}, f32[512,512]{1,0:T(8,128)}, u32[]{:S(2)}) copy-start(f32[512,512]{1,0:T(8,128)} %dadj.1) | copy-start | bytes 3145732
  42.8 2.0 %collective-permute-start.15 = (bf16[640,128]{1,0:T(8,128)(2,1)S(1)}, bf16[640,128]{1,0:T(8,128)(2,1)S(1)}, u32[]{:S(2)}, u32[]{:S(2)}) collective-permute-start(bf16[640,128]{1,0:T(8,128)(2,1)S(1)} %pad_maximum_fusion), channel_id=1, source_target_pairs={{0,8},{8,0},{16,24},{24,16},{1,9},{9,1},{17,25},{25,17},{2,10},{10... | collective-permute-start | bytes 491528 | tf_op jit(solution)/shard_map/ppermute | solution.py:399
  43.4 1.4 %copy-start.6 = (bf16[128,2,1,128]{3,1,2,0:T(2,128)(2,1)S(1)}, bf16[128,2,1,128]{3,1,2,0:T(2,128)(2,1)}, u32[]{:S(2)}) copy-start(bf16[128,2,1,128]{3,1,2,0:T(2,128)(2,1)} %param.16) | copy-start | bytes 196612
  43.4 4.3 %collective-permute-start.17 = (bf16[128,256]{1,0:T(8,128)(2,1)S(1)}, bf16[128,256]{1,0:T(8,128)(2,1)S(1)}, u32[]{:S(2)}, u32[]{:S(2)}) collective-permute-start(bf16[128,256]{1,0:T(8,128)(2,1)S(1)} %fusion.2), channel_id=1, source_target_pairs={{0,16},{8,24},{16,0},{24,8},{1,17},{9,25},{17,1},{25,9},{2,18},{10... | collective-permute-start | bytes 196616 | tf_op jit(solution)/shard_map/ppermute | solution.py:400

commit v3 on v2

--- a/solution.py
+++ b/solution.py
@@ -83,8 +83,11 @@
     )
 
 
-TIES = {'r1': 'sum', 'r2': 'none', 'r3': 'z1sum', 'r4': 'none', 's1': 'z1', 's2': 'z1', 's3': 'z2sum', 's4': 'none', 'pf': 'xsum', 'prep': 'xsum', 'below': 'ag'}
-SPLIT, CUT, LATE, LIM = True, 112, False, 40 * 2**20
+TIES = {'r1': 'sum', 'r2': 'xsum', 'r3': 'z1sum', 'r4': 'none', 's1': 'z1', 's2': 'z1sum', 's3': 'z2sum', 's4': 'none', 'pf': 'z1', 'prep': 'z1sum', 'below': 'ag'}
+SPLIT, CUT, LATE, LIM = True, 112, True, 20 * 2**20
+PAIRED = False
+PREPC = 0
+ONLY = (0, 2)
 VM = pl.BlockSpec(memory_space=pltpu.VMEM)
 ANYM = pl.BlockSpec(memory_space=pl.ANY)
 
@@ -152,27 +155,15 @@
     back.wait()
 
 
-def split(value):
-    high = value.astype(BF)
-    return high, (value - high.astype(F32)).astype(BF)
-
-
-def prep_kernel(fac, inv, fac_t_hi, fac_t_lo, inv_t_hi, inv_t_lo, inv_hi, inv_lo, done):
+def prep_kernel(fac, inv, fac_t, inv_t, inv_bf, done):
     done[...] = jnp.zeros_like(done)
-    fac_t_hi[...], fac_t_lo[...] = split(fac[...].T)
-    inverse = inv[...]
-    inv_t_hi[...], inv_t_lo[...] = split(inverse.T)
-    inv_hi[...], inv_lo[...] = split(inverse)
-
-
-def dot2(a_hi, a_lo, b):
-    d = functools.partial(jnp.dot, preferred_element_type=F32)
-    return d(a_hi, b) + d(a_lo, b)
-
-
-def dot2r(a, b_hi, b_lo):
-    d = functools.partial(jnp.dot, preferred_element_type=F32)
-    return d(a, b_hi) + d(a, b_lo)
+    fac_t[...] = fac[...].T.astype(BF)
+    inv_t[...] = inv[...].T.astype(BF)
+    inv_bf[...] = inv[...].astype(BF)
+
+
+def product(a, b):
+    return jnp.dot(a, b, preferred_element_type=F32)
 
 
 def natural(view, scratch):
@@ -194,7 +185,7 @@
 
 def solve_kernel(
     c_own, c_y, c_core, prior, bar, dadj,
-    fac_t_hi, fac_t_lo, inv_t_hi, inv_t_lo, inv_hi, inv_lo, *others
+    fac_t, inv_t, inv_bf, *others
 ):
     out, rest, cross, full, twice, inter = others[-6:]
     quarter = c_own.shape[0]
@@ -232,17 +223,17 @@
     d_tt = lower(reduced(top, top), 1.0).astype(BF)
     d_lt = reduced(low, top).astype(BF)
     d_ll = lower(reduced(low, low), 1.0).astype(BF)
-    p_tt = dot2(fac_t_hi[top, :], fac_t_lo[top, :], jnp.concatenate([d_tt, d_lt], axis=0))
-    p_l = dot2(
-        fac_t_hi[low, low], fac_t_lo[low, low], jnp.concatenate([d_lt, d_ll], axis=1)
+    p_tt = product(fac_t[top, :], jnp.concatenate([d_tt, d_lt], axis=0))
+    p_l = product(
+        fac_t[low, low], jnp.concatenate([d_lt, d_ll], axis=1)
     )
     f_tt = lower(p_tt, 0.5).astype(BF)
     f_lt = p_l[:, top].astype(BF)
     f_ll = lower(p_l[:, low], 0.5).astype(BF)
-    a_tt = dot2(inv_t_hi[top, :], inv_t_lo[top, :], jnp.concatenate([f_tt, f_lt], axis=0))
-    a_tl = dot2(inv_t_hi[top, low], inv_t_lo[top, low], f_ll)
-    a_l = dot2(
-        inv_t_hi[low, low], inv_t_lo[low, low], jnp.concatenate([f_lt, f_ll], axis=1)
+    a_tt = product(inv_t[top, :], jnp.concatenate([f_tt, f_lt], axis=0))
+    a_tl = product(inv_t[top, low], f_ll)
+    a_l = product(
+        inv_t[low, low], jnp.concatenate([f_lt, f_ll], axis=1)
     )
     left = jnp.concatenate(
         [
@@ -251,8 +242,8 @@
         ],
         axis=0,
     )
-    full[:, top] = dot2r(left, inv_hi[:, top], inv_lo[:, top])
-    full[:, low] = dot2r(left[:, low], inv_hi[low, low], inv_lo[low, low])
+    full[:, top] = product(left, inv_bf[:, top])
+    full[:, low] = product(left[:, low], inv_bf[low, low])
     value = full[...]
     grad = 0.5 * (value + value.T)
     out[...] = grad
@@ -298,14 +289,14 @@
 
 
 def step_kernel(offsets, n, first, *refs):
+    grads, inter = refs[len(offsets) + 5 : -1], refs[-1]
     if first:
-        own, *parts, inv, below, acc = refs[: len(offsets) + 4]
-        grads, inter = refs[len(offsets) + 4 : -1], refs[-1]
+        own, *parts, inv, below, acc, done = refs[: len(offsets) + 5]
         accumulate(own, 0, n, below, inter, acc, True)
     else:
-        *parts, inv, below, before, acc = refs[: len(offsets) + 4]
-        grads, inter = refs[len(offsets) + 4 : -1], refs[-1]
+        *parts, inv, below, before, acc, done = refs[: len(offsets) + 5]
         acc[...] = before[...]
+    done[...] = jnp.zeros_like(done)
     inverse = inv[...].astype(BF)
     for off, part, grad in zip(offsets, parts, grads):
         grad[...] = jnp.dot(part[...], inverse, preferred_element_type=F32).astype(BF)
@@ -418,7 +409,7 @@
     def step_call(name, offs, parts, acc=None):
         return call(
             functools.partial(step_kernel, offs, n_gc, acc is None),
-            [((width, cols), F32)] + [shard] * len(offs),
+            [((width, cols), F32), token] + [shard] * len(offs),
             [*parts, diag_inverse, bf_view] + ([] if acc is None else [acc]),
             scratch=[pltpu.VMEM((shard_rows * ct, cb), F32)],
             name=name,
@@ -449,6 +440,11 @@
 
     to_right = lambda v: lax.ppermute(v, "gc", right)
     to_left = lambda v: lax.ppermute(v, "gc", left)
+    turn = [
+        (g * n_gc + src, g * n_gc + dst)
+        for g in range(n_gr)
+        for src, dst in (right if g % 2 else left)
+    ]
     plus = lambda a, b: (a.astype(F32) + b.astype(F32)).astype(BF)
     y = my_y()
     env = {}
@@ -463,33 +459,50 @@
         elif item in ("r2", "r3"):
             before = "r%d" % (int(item[1]) - 1)
             need(before)
+            step = "s%d" % (int(item[1]) - 1)
+            if TIES[step] == item:
+                need(step)
+                *env[before], env[step][0] = lax.optimization_barrier(
+                    (*env[before], env[step][0])
+                )
             u, v = env[before]
             env[item] = [to_right(u), to_left(v)]
         elif item == "r4":
             need("r3")
+            if TIES["s3"] == item:
+                need("s3")
+                *env["r3"], env["s3"][0] = lax.optimization_barrier(
+                    (*env["r3"], env["s3"][0])
+                )
             u, v = env["r3"]
-            env[item] = [to_right(u[:CUT]), to_left(v[CUT:])] if SPLIT else [to_right(u)]
+            if SPLIT:
+                env[item] = [to_right(u[:CUT]), to_left(v[CUT:])]
+            else:
+                env[item] = [lax.ppermute(jnp.where(my_core() == 1, u, v), ("gr", "gc"), turn)]
         elif item in ("s1", "s2", "s3"):
             k = int(item[1])
             need("r%d" % k)
             if k > 1:
                 need("s%d" % (k - 1))
             lead = [grad] if k == 1 else []
-            acc, *out = step_call(
-                "step_%d" % k, [k, -k], [*lead, *env["r%d" % k]],
-                None if k == 1 else env["s%d" % (k - 1)][0],
+            env["acc"], mark, *out = step_call(
+                "step_%d" % k, [k, -k], [*lead, *env["r%d" % k]], env.get("acc")
             )
-            env[item], env["g%d" % k] = [acc], out
+            env[item], env["g%d" % k] = [mark], out
         elif item == "prep":
             *out, mark = call(
                 prep_kernel,
-                [((width, width), BF)] * 6 + [token],
+                [((width, width), BF)] * 3 + [token],
                 [diag_factor, diag_inverse],
                 name="prep",
+                flops=PREPC,
             )
             env["prepared"], env[item] = out, [mark]
         elif item == "pf":
-            env[item] = [ynb(env["pair"])]
+            if PAIRED:
+                env[item] = [jnp.concatenate([env["pf_y"], core(env["pf_y"])], axis=0)]
+            else:
+                env[item] = [ynb(env["pair"])]
         elif item == "below":
             need("s3")
             need("pf")
@@ -512,7 +525,7 @@
             keep_x, send_x, g4 = call(
                 functools.partial(last_kernel, n_gc // 2, n_gc, len(env["r4"])),
                 [((2, BLK, cols), F32), ((2, BLK, cols), BF), ((shard_rows, width), BF)],
-                [*env["r4"], diag_inverse, bf_view, env["s3"][0]],
+                [*env["r4"], diag_inverse, bf_view, env["acc"]],
                 scratch=[
                     pltpu.VMEM((shard_rows * ct, cb), F32),
                     pltpu.VMEM((width, cols), F32),
@@ -528,12 +541,14 @@
         items = [k for k, v in TIES.items() if v == point]
         for item in items:
             need(item)
-        vals = [v for item in items for v in env[item]]
+        part_of = lambda item: slice(*ONLY) if item == "r1" else slice(None)
+        vals = [v for item in items for v in env[item][part_of(item)]]
         if not vals:
             return value
         value, *vals = lax.optimization_barrier((value, *vals))
         for item in items:
-            env[item] = [vals.pop(0) for _ in env[item]]
+            at = part_of(item)
+            env[item][at] = [vals.pop(0) for _ in env[item][at]]
         return value
 
     got = gate("sum", core(gate("core", send)))
@@ -541,7 +556,13 @@
     mine = lax.dynamic_index_in_dim(both, y, 0, keepdims=False)
     other = lax.dynamic_index_in_dim(both, 1 - y, 0, keepdims=False).astype(BF)
     env["pair"] = jnp.concatenate([pf_view, got[half_rows:]], axis=0)
-    part = plus(mine, gate("ysum", ynb(gate("y", other))))
+    if PAIRED:
+        arrived = ynb(gate("y", jnp.concatenate([other, pf_view], axis=0)))
+        arrived = gate("ysum", arrived)
+        env["pf_y"] = arrived[quarter:]
+        part = plus(mine, arrived[:quarter])
+    else:
+        part = plus(mine, gate("ysum", ynb(gate("y", other))))
     for k, name in enumerate(("x", "z1", "z2")):
         part = gate(name, part)
         part = plus(part, gate(name + "sum", gcx(part, 1 << k)))
@@ -553,7 +574,7 @@
     got_x = ynb(env["s4"][0])
     prepared = env["prepared"]
     below_early, last_bar, prior_whole = env["early"]
-    marks = env["prep"] + env["below"]
+    marks = env["prep"] + env["below"] + env["s1"] + env["s2"] + env["s3"]
     g4 = env["g4"]
     if LATE:
         part_c = tie(part_c, env["s4"][0])
@@ -571,7 +592,7 @@
         flops=18 * width**3,
         nbytes=2**22,
         name="solve",
-        specs=[VM] * 12 + [ANYM] * len(marks),
+        specs=[VM] * 9 + [ANYM] * len(marks),
     )
     (below_new,) = call(
         functools.partial(below_last_kernel, n_gc),

time: 48.6 us -> 47.8 us (0.984)
  waiting for transfers between devices: 14.1 us -> 15.3 us
  starting transfers between devices: 20.2 us -> 19.1 us
  Pallas kernels: 13 us -> 12.1 us
    ppermute x3, waiting for transfers between devices: 6.47 us -> 4.54 us  [local_fast(): gcx = lambda v, bit: lax.ppermute(v, 'gc', xor_perm(n_gc, bit))]
    ppermute x4, waiting for transfers between devices: 4.01 us -> 5.44 us  [local_fast(): to_right = lambda v: lax.ppermute(v, 'gc', right)]
    ppermute x4, waiting for transfers between devices: 0.57 us -> 1.95 us  [local_fast(): ynb = lambda v: lax.ppermute(v, 'gr', xor_perm(n_gr, 2))]
    ppermute x4, starting transfers between devices: 5.4 us -> 4.56 us  [local_fast(): ynb = lambda v: lax.ppermute(v, 'gr', xor_perm(n_gr, 2))]
    pallas_call x10, Pallas kernels: 13 us -> 12.1 us  [call(): pl.pallas_call(body, out_shape=[jax.ShapeDtypeStruct(s, d) for s, d in ou...]
    ppermute x3, starting transfers between devices: 4.85 us -> 4.08 us  [local_fast(): gcx = lambda v, bit: lax.ppermute(v, 'gc', xor_perm(n_gc, bit))]
    ppermute x4, starting transfers between devices: 4.39 us -> 4.96 us  [local_fast(): to_left = lambda v: lax.ppermute(v, 'gc', left)]
  transfers between devices with their start and end apart: 18 -> 18, of which waited for: 9 -> 10; matrix products, arithmetic and copies ran while one was open for 0% -> 0% of each run, Pallas kernels for 25% -> 24%
where the time goes in v3:
time: 47.8 us; the launch traced here: 47.6 us
  starting transfers between devices  19.1 us (40%)
  waiting for transfers between devices  15.3 us (32%)
  Pallas kernels  12.1 us (25%)
  between operations  0.86 us (2%)
    pallas_call x10, Pallas kernels, call(): pl.pallas_call(body, out_shape=[jax.ShapeDtypeStruct(s, d) for s, d in ou...  12.1 us
    ppermute x4, waiting for transfers between devices, local_fast(): to_right = lambda v: lax.ppermute(v, 'gc', right)  5.44 us
    ppermute x4, starting transfers between devices, local_fast(): to_left = lambda v: lax.ppermute(v, 'gc', left)  4.96 us
    ppermute x4, starting transfers between devices, local_fast(): to_right = lambda v: lax.ppermute(v, 'gc', right)  4.82 us
    ppermute x4, starting transfers between devices, local_fast(): ynb = lambda v: lax.ppermute(v, 'gr', xor_perm(n_gr, 2))  4.56 us
    ppermute x3, waiting for transfers between devices, local_fast(): gcx = lambda v, bit: lax.ppermute(v, 'gc', xor_perm(n_gc, bit))  4.54 us
    ppermute x3, starting transfers between devices, local_fast(): gcx = lambda v, bit: lax.ppermute(v, 'gc', xor_perm(n_gc, bit))  4.08 us
    ppermute x4, waiting for transfers between devices, local_fast(): ynb = lambda v: lax.ppermute(v, 'gr', xor_perm(n_gr, 2))  1.95 us
  transfers between devices with their start and end apart: 18, of which 10 were waited for; matrix products, arithmetic and copies ran while one was open for 0% of the time, Pallas kernels for 24%

profile of v3, /device:TPU:0, one launch (start us, length us, event | category | flops | bytes accessed | tf_op | source)
XLA Modules:
  0.0 47.6 jit_solution(16261535338530187498)
XLA Ops:
  0.6 3.1 %collective-permute-start.1 = (bf16[248,512]{1,0:T(8,128)(2,1)}, bf16[248,512]{1,0:T(8,128)(2,1)S(1)}, u32[]{:S(2)}, u32[]{:S(2)}) collective-permute-start(bf16[248,512]{1,0:T(8,128)(2,1)} %bitcast.39), channel_id=1, source_target_pairs={{0,2},{2,4},{4,6},{6,7},{7,5},{5,3},{3,1},{1,0},{8,10},{10,12},{12... | collective-permute-start | bytes 761864 | tf_op jit(solution)/shard_map/ppermute | solution.py:441
  3.7 0.0 collective-permute-start.2
  3.7 0.0 copy-start.1
  3.7 2.5 %panel_grad.1 = (bf16[248,512]{1,0:T(8,128)(2,1)}, f32[640,128]{1,0:T(8,128)S(1)}, bf16[896,128]{1,0:T(8,128)(2,1)S(1)}) custom-call(bf16[248,512]{1,0:T(8,128)(2,1)} %bitcast.41, bf16[248,512]{1,0:T(8,128)(2,1)} %bitcast.38, f32[512,512]{1,0:T(8,128)} %refs_2_.5, bf16[256,128]{1,0:T(8,128)(2,1)} %bitcast.36), custom_call_target="tpu_custom_call" | custom-call | tf_op jit(solution)/shard_map/panel_grad/pallas_call | solution.py:97
  6.2 0.0 copy-start
  6.2 0.1 collective-permute-start
  6.3 1.5 %collective-permute-done = bf16[896,128]{1,0:T(8,128)(2,1)S(1)} collective-permute-done((bf16[896,128]{1,0:T(8,128)(2,1)S(1)}, bf16[896,128]{1,0:T(8,128)(2,1)S(1)}, u32[]{:S(2)}, u32[]{:S(2)}) %collective-permute-start) | collective-permute-done | bytes 229408 | tf_op jit(solution)/shard_map/ppermute | solution.py:390
  7.8 2.2 %collective-permute-done.1.refs_1_ = bf16[248,512]{1,0:T(8,128)(2,1)S(1)} collective-permute-done((bf16[248,512]{1,0:T(8,128)(2,1)}, bf16[248,512]{1,0:T(8,128)(2,1)S(1)}, u32[]{:S(2)}, u32[]{:S(2)}) %collective-permute-start.1) | collective-permute-done | bytes 253984 | tf_op jit(solution)/shard_map/ppermute | solution.py:441
  10.0 1.5 %collective-permute-done.2.refs_2_ = bf16[248,512]{1,0:T(8,128)(2,1)S(1)} collective-permute-done((bf16[248,512]{1,0:T(8,128)(2,1)}, bf16[248,512]{1,0:T(8,128)(2,1)S(1)}, u32[]{:S(2)}, u32[]{:S(2)}) %collective-permute-start.2) | collective-permute-done | bytes 253984 | tf_op jit(solution)/shard_map/ppermute | solution.py:442
  11.6 1.6 %collective-permute-start.3 = (bf16[320,128]{1,0:T(8,128)(2,1)S(1)}, bf16[320,128]{1,0:T(8,128)(2,1)S(1)}, u32[]{:S(2)}, u32[]{:S(2)}) collective-permute-start(bf16[320,128]{1,0:T(8,128)(2,1)S(1)} %fusion.1), channel_id=1, source_target_pairs={{0,16},{8,24},{16,0},{24,8},{1,17},{9,25},{17,1},{25,9},{2,18},{10... | collective-permute-start | bytes 245768 | tf_op jit(solution)/shard_map/ppermute | solution.py:391
  13.2 0.0 copy-start.7
  13.2 0.0 copy-start.4
  13.2 1.6 %collective-permute-start.5 = (bf16[248,512]{1,0:T(8,128)(2,1)S(1)}, bf16[248,512]{1,0:T(8,128)(2,1)S(1)}, u32[]{:S(2)}, u32[]{:S(2)}) collective-permute-start(bf16[248,512]{1,0:T(8,128)(2,1)S(1)} %collective-permute-done.1.refs_1_), channel_id=1, source_target_pairs={{0,2},{2,4},{4,6},{6,7},{7,5},{5,3},{3,1},{1,0},{8,10},{10,12},{12... | collective-permute-start | bytes 761864 | tf_op jit(solution)/shard_map/ppermute | solution.py:441
  14.8 0.4 collective-permute-start.6
  15.2 0.8 %collective-permute-done.3 = bf16[320,128]{1,0:T(8,128)(2,1)S(1)} collective-permute-done((bf16[320,128]{1,0:T(8,128)(2,1)S(1)}, bf16[320,128]{1,0:T(8,128)(2,1)S(1)}, u32[]{:S(2)}, u32[]{:S(2)}) %collective-permute-start.3) | collective-permute-done | bytes 81952 | tf_op jit(solution)/shard_map/ppermute | solution.py:391
  16.1 0.4 collective-permute-start.4
  16.5 0.0 copy-done.7
  16.5 1.7 %collective-permute-start.7 = (bf16[512,128]{1,0:T(8,128)(2,1)S(1)}, bf16[512,128]{1,0:T(8,128)(2,1)S(1)}, u32[]{:S(2)}, u32[]{:S(2)}) collective-permute-start(bf16[512,128]{1,0:T(8,128)(2,1)S(1)} %pad_maximum_fusion.1.refs_7_), channel_id=1, source_target_pairs={{0,16},{8,24},{16,0},{24,8},{1,17},{9,25},{17,1},{25,9},{2,18},{10... | collective-permute-start | bytes 393224 | tf_op jit(solution)/shard_map/ppermute | solution.py:391
  18.2 0.0 copy-done.1
  18.2 0.0 copy-done
  18.2 0.0 copy-done.4
  18.2 0.0 copy-start.2
  18.2 0.9 %step_1.1 = (f32[512,256]{1,0:T(8,128)S(1)}, f32[8,128]{1,0:T(8,128)S(1)}, bf16[248,512]{1,0:T(8,128)(2,1)S(1)}, bf16[248,512]{1,0:T(8,128)(2,1)S(1)}) custom-call(bf16[248,512]{1,0:T(8,128)(2,1)S(1)} %copy-done.4, bf16[248,512]{1,0:T(8,128)(2,1)S(1)} %collective-permute-done.1.refs_1_, bf16[248,512]{1,0:T(8,128)(2,1)S(1)} %collective-permute-done.2.refs_2_, ...), custom_call_target="tpu_custom_call" | custom-call | tf_op jit(solution)/shard_map/step_1/pallas_call | solution.py:97
  19.2 2.2 %collective-permute-done.4 = bf16[320,128]{1,0:T(8,128)(2,1)S(1)} collective-permute-done((bf16[320,128]{1,0:T(8,128)(2,1)S(1)}, bf16[320,128]{1,0:T(8,128)(2,1)S(1)}, u32[]{:S(2)}, u32[]{:S(2)}) %collective-permute-start.4) | collective-permute-done | bytes 81952 | tf_op jit(solution)/shard_map/ppermute | solution.py:392
  21.4 0.0 collective-permute-done.5.refs_0_
  21.4 0.0 collective-permute-done.6.refs_1_
  21.4 1.9 %collective-permute-start.10 = (bf16[248,512]{1,0:T(8,128)(2,1)S(1)}, bf16[248,512]{1,0:T(8,128)(2,1)S(1)}, u32[]{:S(2)}, u32[]{:S(2)}) collective-permute-start(bf16[248,512]{1,0:T(8,128)(2,1)S(1)} %collective-permute-done.6.refs_1_), channel_id=1, source_target_pairs={{2,0},{4,2},{6,4},{7,6},{5,7},{3,5},{1,3},{0,1},{10,8},{12,10},{14... | collective-permute-start | bytes 761864 | tf_op jit(solution)/shard_map/ppermute | solution.py:442
  23.3 0.1 collective-permute-start.9
  23.4 0.0 collective-permute-done.7.refs_8_
  23.5 1.4 %collective-permute-start.8 = (bf16[320,128]{1,0:T(8,128)(2,1)S(1)}, bf16[320,128]{1,0:T(8,128)(2,1)S(1)}, u32[]{:S(2)}, u32[]{:S(2)}) collective-permute-start(bf16[320,128]{1,0:T(8,128)(2,1)S(1)} %add_convert_fusion.2), channel_id=1, source_target_pairs={{0,2},{1,3},{2,0},{3,1},{4,6},{5,7},{6,4},{7,5},{8,10},{9,11},{10,... | collective-permute-start | bytes 245768 | tf_op jit(solution)/shard_map/ppermute | solution.py:392
  24.9 0.0 copy-done.2
  24.9 0.3 prep.1
  25.2 1.0 %step_2.1 = (f32[512,256]{1,0:T(8,128)S(1)}, f32[8,128]{1,0:T(8,128)S(1)}, bf16[248,512]{1,0:T(8,128)(2,1)S(1)}, bf16[248,512]{1,0:T(8,128)(2,1)S(1)}) custom-call(bf16[248,512]{1,0:T(8,128)(2,1)S(1)} %collective-permute-done.5.refs_0_, bf16[248,512]{1,0:T(8,128)(2,1)S(1)} %collective-permute-done.6.refs_1_, f32[512,512]{1,0:T(8,128)S(1)} %copy-done, ...), custom_call_target="tpu_custom_call" | custom-call | tf_op jit(solution)/shard_map/step_2/pallas_call | solution.py:97
  26.3 2.3 %collective-permute-done.8 = bf16[320,128]{1,0:T(8,128)(2,1)S(1)} collective-permute-done((bf16[320,128]{1,0:T(8,128)(2,1)S(1)}, bf16[320,128]{1,0:T(8,128)(2,1)S(1)}, u32[]{:S(2)}, u32[]{:S(2)}) %collective-permute-start.8) | collective-permute-done | bytes 81952 | tf_op jit(solution)/shard_map/ppermute | solution.py:392
  28.6 0.0 collective-permute-done.10.refs_1_
  28.6 1.0 %collective-permute-done.9.refs_0_ = bf16[248,512]{1,0:T(8,128)(2,1)S(1)} collective-permute-done((bf16[248,512]{1,0:T(8,128)(2,1)S(1)}, bf16[248,512]{1,0:T(8,128)(2,1)S(1)}, u32[]{:S(2)}, u32[]{:S(2)}) %collective-permute-start.9) | collective-permute-done | bytes 253984 | tf_op jit(solution)/shard_map/ppermute | solution.py:441
  29.6 2.2 %collective-permute-start.13 = (bf16[320,128]{1,0:T(8,128)(2,1)S(1)}, bf16[320,128]{1,0:T(8,128)(2,1)S(1)}, u32[]{:S(2)}, u32[]{:S(2)}) collective-permute-start(bf16[320,128]{1,0:T(8,128)(2,1)S(1)} %add_convert_fusion.1), channel_id=1, source_target_pairs={{0,4},{1,5},{2,6},{3,7},{4,0},{5,1},{6,2},{7,3},{8,12},{9,13},{10,... | collective-permute-start | bytes 245768 | tf_op jit(solution)/shard_map/ppermute | solution.py:392
  31.9 0.0 copy-start.3
  31.9 1.0 %step_3.1 = (f32[512,256]{1,0:T(8,128)S(1)}, f32[8,128]{1,0:T(8,128)S(1)}, bf16[248,512]{1,0:T(8,128)(2,1)S(1)}, bf16[248,512]{1,0:T(8,128)(2,1)S(1)}) custom-call(bf16[248,512]{1,0:T(8,128)(2,1)S(1)} %collective-permute-done.9.refs_0_, bf16[248,512]{1,0:T(8,128)(2,1)S(1)} %collective-permute-done.10.refs_1_, f32[512,512]{1,0:T(8,128)S(1)} %copy-done, ...), custom_call_target="tpu_custom_call" | custom-call | tf_op jit(solution)/shard_map/step_3/pallas_call | solution.py:97
  33.0 2.6 %collective-permute-start.12 = (bf16[136,512]{1,0:T(8,128)(2,1)S(1)}, bf16[136,512]{1,0:T(8,128)(2,1)S(1)}, u32[]{:S(2)}, u32[]{:S(2)}) collective-permute-start(bf16[136,512]{1,0:T(8,128)(2,1)S(1)} %slice.15), channel_id=1, source_target_pairs={{2,0},{4,2},{6,4},{7,6},{5,7},{3,5},{1,3},{0,1},{10,8},{12,10},{14... | collective-permute-start | bytes 417800 | tf_op jit(solution)/shard_map/ppermute | solution.py:442
  35.5 0.0 collective-permute-start.11
  35.5 0.0 copy-done.3
  35.6 1.8 %below_early.1 = (bf16[31,8,16,128]{3,2,1,0:T(8,128)(2,1)}, bf16[496,128]{1,0:T(8,128)(2,1)S(1)}, bf16[512,256]{1,0:T(8,128)(2,1)S(1)}, f32[8,128]{1,0:T(8,128)S(1)}) custom-call(bf16[248,512]{1,0:T(8,128)(2,1)S(1)} %copy-done.4, bf16[248,512]{1,0:T(8,128)(2,1)S(1)} %get-tuple-element.55.refs_1_, bf16[248,512]{1,0:T(8,128)(2,1)S(1)} %get-tuple-element.56.refs_2_, ...), custom_call_target="tpu_custom_call" | custom-call | tf_op jit(solution)/shard_map/below_early/pallas_call | solution.py:97
  37.4 0.0 collective-permute-done.13
  37.4 0.6 %collective-permute-start.14 = (bf16[320,128]{1,0:T(8,128)(2,1)S(1)}, bf16[320,128]{1,0:T(8,128)(2,1)S(1)}, u32[]{:S(2)}, u32[]{:S(2)}) collective-permute-start(bf16[320,128]{1,0:T(8,128)(2,1)S(1)} %add_convert_fusion.c_own), channel_id=1, source_target_pairs={{0,16},{8,24},{16,0},{24,8},{1,17},{9,25},{17,1},{25,9},{2,18},{10... | collective-permute-start | bytes 245768 | tf_op jit(solution)/shard_map/ppermute | solution.py:391
  38.1 2.3 %collective-permute-done.11.refs_0_ = bf16[112,512]{1,0:T(8,128)(2,1)S(1)} collective-permute-done((bf16[112,512]{1,0:T(8,128)(2,1)S(1)}, bf16[112,512]{1,0:T(8,128)(2,1)S(1)}, u32[]{:S(2)}, u32[]{:S(2)}) %collective-permute-start.11) | collective-permute-done | bytes 114720 | tf_op jit(solution)/shard_map/ppermute | solution.py:441
  40.3 0.0 collective-permute-done.12.refs_1_
  40.3 0.6 %step_four.1 = (f32[2,128,256]{2,1,0:T(8,128)S(1)}, bf16[2,128,256]{2,1,0:T(8,128)(2,1)S(1)}, bf16[248,512]{1,0:T(8,128)(2,1)S(1)}) custom-call(bf16[112,512]{1,0:T(8,128)(2,1)S(1)} %collective-permute-done.11.refs_0_, bf16[136,512]{1,0:T(8,128)(2,1)S(1)} %collective-permute-done.12.refs_1_, f32[512,512]{1,0:T(8,128)S(1)} %copy-done, ...), custom_call_target="tpu_custom_call" | custom-call | tf_op jit(solution)/shard_map/step_four/pallas_call | solution.py:97
  41.0 0.1 collective-permute-start.16
  41.1 0.9 %below_last.1 = bf16[31,8,16,128]{3,2,1,0:T(8,128)(2,1)} custom-call(bf16[31,8,16,128]{3,2,1,0:T(8,128)(2,1)} %get-tuple-element.75.early, bf16[248,512]{1,0:T(8,128)(2,1)S(1)} %get-tuple-element.77.grad, bf16[512,256]{1,0:T(8,128)(2,1)S(1)} %get-tuple-element.78.whole.prior, bf16[496,128]{1,0:T(8,128)(2,1)S(1)} %get-tuple-element.79.bar), custom_call_target="tpu_custom_call", output_to_operand_aliasing={{}: (0, {})} | custom-call | tf_op jit(solution)/shard_map/below_last/pallas_call | solution.py:97
  42.0 0.0 copy-start.5
  42.0 0.0 collective-permute-done.14.c_y
  42.0 0.6 %collective-permute-start.15 = (bf16[640,128]{1,0:T(8,128)(2,1)S(1)}, bf16[640,128]{1,0:T(8,128)(2,1)S(1)}, u32[]{:S(2)}, u32[]{:S(2)}) collective-permute-start(bf16[640,128]{1,0:T(8,128)(2,1)S(1)} %pad_maximum_fusion), channel_id=1, source_target_pairs={{0,8},{8,0},{16,24},{24,16},{1,9},{9,1},{17,25},{25,17},{2,10},{10... | collective-permute-start | bytes 491528 | tf_op jit(solution)/shard_map/ppermute | solution.py:390
  42.6 0.0 collective-permute-done.16
  42.6 0.0 copy-start.6
  42.7 0.6 %collective-permute-start.17 = (bf16[128,256]{1,0:T(8,128)(2,1)S(1)}, bf16[128,256]{1,0:T(8,128)(2,1)S(1)}, u32[]{:S(2)}, u32[]{:S(2)}) collective-permute-start(bf16[128,256]{1,0:T(8,128)(2,1)S(1)} %fusion.2), channel_id=1, source_target_pairs={{0,16},{8,24},{16,0},{24,8},{1,17},{9,25},{17,1},{25,9},{2,18},{10... | collective-permute-start | bytes 196616 | tf_op jit(solution)/shard_map/ppermute | solution.py:391
  43.3 0.3 collective-permute-done.15.c_core
  43.6 0.0 copy-done.5
  43.6 0.0 copy-done.6
  43.6 2.2 %solve.1 = (f32[512,512]{1,0:T(8,128)}, f32[128,256]{1,0:T(8,128)S(1)}) custom-call(bf16[320,128]{1,0:T(8,128)(2,1)S(1)} %add_convert_fusion.c_own, bf16[320,128]{1,0:T(8,128)(2,1)S(1)} %collective-permute-done.14.c_y, bf16[640,128]{1,0:T(8,128)(2,1)S(1)} %collective-permute-done.15.c_core, bf16[512,256]{1,0:T(8,128)(2,1)S(1)} %get-tuple-element.78.whole.prior, ...), custom_call_target="tpu_custom_call" | custom-call | flops 2415919104 | bytes 4194304 | tf_op jit(solution)/shard_map/solve/pallas_call | solution.py:97
  45.9 1.1 %collective-permute-done.17.recv = bf16[128,256]{1,0:T(8,128)(2,1)S(1)} collective-permute-done((bf16[128,256]{1,0:T(8,128)(2,1)S(1)}, bf16[128,256]{1,0:T(8,128)(2,1)S(1)}, u32[]{:S(2)}, u32[]{:S(2)}) %collective-permute-start.17) | collective-permute-done | bytes 65568 | tf_op jit(solution)/shard_map/ppermute | solution.py:391
  47.0 0.7 %prior_sum.1 = bf16[256,128]{1,0:T(8,128)(2,1)} custom-call(f32[128,256]{1,0:T(8,128)S(1)} %get-tuple-element.96.rest, f32[128,256]{1,0:T(8,128)S(1)} %dynamic-slice_bitcast_fusion.keep, bf16[128,256]{1,0:T(8,128)(2,1)S(1)} %collective-permute-done.17.recv), custom_call_target="tpu_custom_call" | custom-call | flops 327680 | bytes 262144 | tf_op jit(solution)/shard_map/prior_sum/pallas_call | solution.py:97
  (14 shorter events, 0.2 us)
Async XLA Ops:
  0.6 9.3 %collective-permute-start.1 = (bf16[248,512]{1,0:T(8,128)(2,1)}, bf16[248,512]{1,0:T(8,128)(2,1)S(1)}, u32[]{:S(2)}, u32[]{:S(2)}) collective-permute-start(bf16[248,512]{1,0:T(8,128)(2,1)} %bitcast.39), channel_id=1, source_target_pairs={{0,2},{2,4},{4,6},{6,7},{7,5},{5,3},{3,1},{1,0},{8,10},{10,12},{12... | collective-permute-start | bytes 761864 | tf_op jit(solution)/shard_map/ppermute | solution.py:441
  3.7 7.8 %collective-permute-start.2 = (bf16[248,512]{1,0:T(8,128)(2,1)}, bf16[248,512]{1,0:T(8,128)(2,1)S(1)}, u32[]{:S(2)}, u32[]{:S(2)}) collective-permute-start(bf16[248,512]{1,0:T(8,128)(2,1)} %bitcast.40), channel_id=1, source_target_pairs={{2,0},{4,2},{6,4},{7,6},{5,7},{3,5},{1,3},{0,1},{10,8},{12,10},{14... | collective-permute-start | bytes 761864 | tf_op jit(solution)/shard_map/ppermute | solution.py:442
  3.7 14.5 %copy-start.1 = (bf16[31,1,64,2,1,128]{5,3,4,2,1,0:T(2,128)(2,1)S(1)}, bf16[31,1,64,2,1,128]{5,3,4,2,1,0:T(2,128)(2,1)}, u32[]{:S(2)}) copy-start(bf16[31,1,64,2,1,128]{5,3,4,2,1,0:T(2,128)(2,1)} %param.9) | copy-start | bytes 3047428
  6.2 12.0 %copy-start = (f32[512,512]{1,0:T(8,128)S(1)}, f32[512,512]{1,0:T(8,128)}, u32[]{:S(2)}) copy-start(f32[512,512]{1,0:T(8,128)} %refs_2_.5) | copy-start | bytes 3145732
  6.2 1.6 %collective-permute-start = (bf16[896,128]{1,0:T(8,128)(2,1)S(1)}, bf16[896,128]{1,0:T(8,128)(2,1)S(1)}, u32[]{:S(2)}, u32[]{:S(2)}) collective-permute-start(bf16[896,128]{1,0:T(8,128)(2,1)S(1)} %get-tuple-element.52), channel_id=1, source_target_pairs={{0,8},{8,0},{16,24},{24,16},{1,9},{9,1},{17,25},{25,17},{2,10},{10... | collective-permute-start | bytes 688136 | tf_op jit(solution)/shard_map/ppermute | solution.py:390
  11.6 4.5 %collective-permute-start.3 = (bf16[320,128]{1,0:T(8,128)(2,1)S(1)}, bf16[320,128]{1,0:T(8,128)(2,1)S(1)}, u32[]{:S(2)}, u32[]{:S(2)}) collective-permute-start(bf16[320,128]{1,0:T(8,128)(2,1)S(1)} %fusion.1), channel_id=1, source_target_pairs={{0,16},{8,24},{16,0},{24,8},{1,17},{9,25},{17,1},{25,9},{2,18},{10... | collective-permute-start | bytes 245768 | tf_op jit(solution)/shard_map/ppermute | solution.py:391
  13.2 3.3 %copy-start.7 = (bf16[128,2,1,128]{3,1,2,0:T(2,128)(2,1)S(1)}, bf16[128,2,1,128]{3,1,2,0:T(2,128)(2,1)}, u32[]{:S(2)}) copy-start(bf16[128,2,1,128]{3,1,2,0:T(2,128)(2,1)} %param.11) | copy-start | bytes 196612
  13.2 5.1 %copy-start.4 = (bf16[248,512]{1,0:T(8,128)(2,1)S(1)}, bf16[248,512]{1,0:T(8,128)(2,1)}, u32[]{:S(2)}) copy-start(bf16[248,512]{1,0:T(8,128)(2,1)} %get-tuple-element.51.refs_0_) | copy-start | bytes 761860
  13.2 8.2 %collective-permute-start.5 = (bf16[248,512]{1,0:T(8,128)(2,1)S(1)}, bf16[248,512]{1,0:T(8,128)(2,1)S(1)}, u32[]{:S(2)}, u32[]{:S(2)}) collective-permute-start(bf16[248,512]{1,0:T(8,128)(2,1)S(1)} %collective-permute-done.1.refs_1_), channel_id=1, source_target_pairs={{0,2},{2,4},{4,6},{6,7},{7,5},{5,3},{3,1},{1,0},{8,10},{10,12},{12... | collective-permute-start | bytes 761864 | tf_op jit(solution)/shard_map/ppermute | solution.py:441
  14.8 6.6 %collective-permute-start.6 = (bf16[248,512]{1,0:T(8,128)(2,1)S(1)}, bf16[248,512]{1,0:T(8,128)(2,1)S(1)}, u32[]{:S(2)}, u32[]{:S(2)}) collective-permute-start(bf16[248,512]{1,0:T(8,128)(2,1)S(1)} %collective-permute-done.2.refs_2_), channel_id=1, source_target_pairs={{2,0},{4,2},{6,4},{7,6},{5,7},{3,5},{1,3},{0,1},{10,8},{12,10},{14... | collective-permute-start | bytes 761864 | tf_op jit(solution)/shard_map/ppermute | solution.py:442
  16.1 5.3 %collective-permute-start.4 = (bf16[320,128]{1,0:T(8,128)(2,1)S(1)}, bf16[320,128]{1,0:T(8,128)(2,1)S(1)}, u32[]{:S(2)}, u32[]{:S(2)}) collective-permute-start(bf16[320,128]{1,0:T(8,128)(2,1)S(1)} %fusion), channel_id=1, source_target_pairs={{0,1},{1,0},{2,3},{3,2},{4,5},{5,4},{6,7},{7,6},{8,9},{9,8},{10,11... | collective-permute-start | bytes 245768 | tf_op jit(solution)/shard_map/ppermute | solution.py:392
  16.5 6.9 %collective-permute-start.7 = (bf16[512,128]{1,0:T(8,128)(2,1)S(1)}, bf16[512,128]{1,0:T(8,128)(2,1)S(1)}, u32[]{:S(2)}, u32[]{:S(2)}) collective-permute-start(bf16[512,128]{1,0:T(8,128)(2,1)S(1)} %pad_maximum_fusion.1.refs_7_), channel_id=1, source_target_pairs={{0,16},{8,24},{16,0},{24,8},{1,17},{9,25},{17,1},{25,9},{2,18},{10... | collective-permute-start | bytes 393224 | tf_op jit(solution)/shard_map/ppermute | solution.py:391
  18.2 6.7 %copy-start.2 = (f32[512,512]{1,0:T(8,128)S(1)}, f32[512,512]{1,0:T(8,128)}, u32[]{:S(2)}) copy-start(f32[512,512]{1,0:T(8,128)} %fac.1) | copy-start | bytes 3145732
  21.4 7.2 %collective-permute-start.10 = (bf16[248,512]{1,0:T(8,128)(2,1)S(1)}, bf16[248,512]{1,0:T(8,128)(2,1)S(1)}, u32[]{:S(2)}, u32[]{:S(2)}) collective-permute-start(bf16[248,512]{1,0:T(8,128)(2,1)S(1)} %collective-permute-done.6.refs_1_), channel_id=1, source_target_pairs={{2,0},{4,2},{6,4},{7,6},{5,7},{3,5},{1,3},{0,1},{10,8},{12,10},{14... | collective-permute-start | bytes 761864 | tf_op jit(solution)/shard_map/ppermute | solution.py:442
  23.3 6.3 %collective-permute-start.9 = (bf16[248,512]{1,0:T(8,128)(2,1)S(1)}, bf16[248,512]{1,0:T(8,128)(2,1)S(1)}, u32[]{:S(2)}, u32[]{:S(2)}) collective-permute-start(bf16[248,512]{1,0:T(8,128)(2,1)S(1)} %collective-permute-done.5.refs_0_), channel_id=1, source_target_pairs={{0,2},{2,4},{4,6},{6,7},{7,5},{5,3},{3,1},{1,0},{8,10},{10,12},{12... | collective-permute-start | bytes 761864 | tf_op jit(solution)/shard_map/ppermute | solution.py:441
  23.5 5.2 %collective-permute-start.8 = (bf16[320,128]{1,0:T(8,128)(2,1)S(1)}, bf16[320,128]{1,0:T(8,128)(2,1)S(1)}, u32[]{:S(2)}, u32[]{:S(2)}) collective-permute-start(bf16[320,128]{1,0:T(8,128)(2,1)S(1)} %add_convert_fusion.2), channel_id=1, source_target_pairs={{0,2},{1,3},{2,0},{3,1},{4,6},{5,7},{6,4},{7,5},{8,10},{9,11},{10,... | collective-permute-start | bytes 245768 | tf_op jit(solution)/shard_map/ppermute | solution.py:392
  29.6 7.8 %collective-permute-start.13 = (bf16[320,128]{1,0:T(8,128)(2,1)S(1)}, bf16[320,128]{1,0:T(8,128)(2,1)S(1)}, u32[]{:S(2)}, u32[]{:S(2)}) collective-permute-start(bf16[320,128]{1,0:T(8,128)(2,1)S(1)} %add_convert_fusion.1), channel_id=1, source_target_pairs={{0,4},{1,5},{2,6},{3,7},{4,0},{5,1},{6,2},{7,3},{8,12},{9,13},{10,... | collective-permute-start | bytes 245768 | tf_op jit(solution)/shard_map/ppermute | solution.py:392
  31.9 3.7 %copy-start.3 = (bf16[31,1,64,2,1,128]{5,3,4,2,1,0:T(2,128)(2,1)S(1)}, bf16[31,1,64,2,1,128]{5,3,4,2,1,0:T(2,128)(2,1)}, u32[]{:S(2)}) copy-start(bf16[31,1,64,2,1,128]{5,3,4,2,1,0:T(2,128)(2,1)} %param.14) | copy-start | bytes 3047428
  33.0 7.4 %collective-permute-start.12 = (bf16[136,512]{1,0:T(8,128)(2,1)S(1)}, bf16[136,512]{1,0:T(8,128)(2,1)S(1)}, u32[]{:S(2)}, u32[]{:S(2)}) collective-permute-start(bf16[136,512]{1,0:T(8,128)(2,1)S(1)} %slice.15), channel_id=1, source_target_pairs={{2,0},{4,2},{6,4},{7,6},{5,7},{3,5},{1,3},{0,1},{10,8},{12,10},{14... | collective-permute-start | bytes 417800 | tf_op jit(solution)/shard_map/ppermute | solution.py:442
  35.5 4.8 %collective-permute-start.11 = (bf16[112,512]{1,0:T(8,128)(2,1)S(1)}, bf16[112,512]{1,0:T(8,128)(2,1)S(1)}, u32[]{:S(2)}, u32[]{:S(2)}) collective-permute-start(bf16[112,512]{1,0:T(8,128)(2,1)S(1)} %slice.14), channel_id=1, source_target_pairs={{0,2},{2,4},{4,6},{6,7},{7,5},{5,3},{3,1},{1,0},{8,10},{10,12},{12... | collective-permute-start | bytes 344072 | tf_op jit(solution)/shard_map/ppermute | solution.py:441
  37.4 4.6 %collective-permute-start.14 = (bf16[320,128]{1,0:T(8,128)(2,1)S(1)}, bf16[320,128]{1,0:T(8,128)(2,1)S(1)}, u32[]{:S(2)}, u32[]{:S(2)}) collective-permute-start(bf16[320,128]{1,0:T(8,128)(2,1)S(1)} %add_convert_fusion.c_own), channel_id=1, source_target_pairs={{0,16},{8,24},{16,0},{24,8},{1,17},{9,25},{17,1},{25,9},{2,18},{10... | collective-permute-start | bytes 245768 | tf_op jit(solution)/shard_map/ppermute | solution.py:391
  41.0 1.6 %collective-permute-start.16 = (bf16[2,128,256]{2,1,0:T(8,128)(2,1)S(1)}, bf16[2,128,256]{2,1,0:T(8,128)(2,1)S(1)}, u32[]{:S(2)}, u32[]{:S(2)}) collective-permute-start(bf16[2,128,256]{2,1,0:T(8,128)(2,1)S(1)} %get-tuple-element.86), channel_id=1, source_target_pairs={{0,8},{8,0},{16,24},{24,16},{1,9},{9,1},{17,25},{25,17},{2,10},{10... | collective-permute-start | bytes 393224 | tf_op jit(solution)/shard_map/ppermute | solution.py:390
  42.0 1.6 %copy-start.5 = (f32[512,512]{1,0:T(8,128)S(1)}, f32[512,512]{1,0:T(8,128)}, u32[]{:S(2)}) copy-start(f32[512,512]{1,0:T(8,128)} %dadj.1) | copy-start | bytes 3145732
  42.0 1.6 %collective-permute-start.15 = (bf16[640,128]{1,0:T(8,128)(2,1)S(1)}, bf16[640,128]{1,0:T(8,128)(2,1)S(1)}, u32[]{:S(2)}, u32[]{:S(2)}) collective-permute-start(bf16[640,128]{1,0:T(8,128)(2,1)S(1)} %pad_maximum_fusion), channel_id=1, source_target_pairs={{0,8},{8,0},{16,24},{24,16},{1,9},{9,1},{17,25},{25,17},{2,10},{10... | collective-permute-start | bytes 491528 | tf_op jit(solution)/shard_map/ppermute | solution.py:390
  42.6 1.0 %copy-start.6 = (bf16[128,2,1,128]{3,1,2,0:T(2,128)(2,1)S(1)}, bf16[128,2,1,128]{3,1,2,0:T(2,128)(2,1)}, u32[]{:S(2)}) copy-start(bf16[128,2,1,128]{3,1,2,0:T(2,128)(2,1)} %param.16) | copy-start | bytes 196612
  42.7 4.3 %collective-permute-start.17 = (bf16[128,256]{1,0:T(8,128)(2,1)S(1)}, bf16[128,256]{1,0:T(8,128)(2,1)S(1)}, u32[]{:S(2)}, u32[]{:S(2)}) collective-permute-start(bf16[128,256]{1,0:T(8,128)(2,1)S(1)} %fusion.2), channel_id=1, source_target_pairs={{0,16},{8,24},{16,0},{24,8},{1,17},{9,25},{17,1},{25,9},{2,18},{10... | collective-permute-start | bytes 196616 | tf_op jit(solution)/shard_map/ppermute | solution.py:391
